TPU v7x, 512 devices: a whole 4x4x16 slice. The times are simulated.
512 devices in a mesh: row: 16 (over y, x), col: 32 (over z, core).
Axes of the slice: x: 4, y: 4, z: 16, core: 2. Of those that a mesh axis runs over, the one named last changes fastest.
Arguments:
- tensor: float32 [32, 4096, 4096], P(None, 'row', 'col'), may hold values from -82 to 82
- old_factor: float32 [4096, 32], P('row'), may hold values from -0.09375 to 0.09375
- factor_two: float32 [4096, 32], P('col'), may hold values from -0.09375 to 0.09375
- factor_three: float32 [32, 32], replicated, may hold values from -1 to 1
Outputs:
- new_factor: float32 [4096, 32], P('row')
- core: float32 [32, 1024], P(None, 'col')
All inputs are finite; a program needn't handle non-finite values.
Results may differ from a plain program's by a relative error of at most 0.0003.
Values sent between devices are 32-bit elements; how exact they have to be, the bound alone decides.
No kernel may reach another device: no remote copies, remote signals or barrier semaphores. Data moves between devices by JAX's collectives and lax.ppermute only.
A program may use at most 64 MiB of HBM per device.

v0:
```python
import math

import jax
import jax.numpy as jnp
from jax import lax
from jax.sharding import PartitionSpec as P

I1 = 4096
ITERS = 2


def right_solve(lower, matrix):
    return lax.linalg.triangular_solve(lower, matrix, left_side=False, lower=True, transpose_a=True)


def shards(tensor, old_factor, factor_two, factor_three):
    highest = lax.Precision.HIGHEST
    depth, rows, cols = tensor.shape
    rank = factor_three.shape[1]
    third = jnp.dot(factor_three.T, tensor.reshape(depth, rows * cols), precision=highest)
    third = third.reshape(rank, rows, cols)
    partial_value = jnp.einsum("bij,ja->iab", third, factor_two, precision=highest).reshape(
        rows, rank * rank
    )
    unfolded = lax.psum_scatter(partial_value, "col", scatter_dimension=1, tiled=True)

    def project(factor):
        local = jnp.dot(unfolded.T, factor, precision=highest)
        summed = lax.psum(local, "row")
        return summed

    factor = old_factor
    coeffs = project(factor)
    for step in range(ITERS):
        image_local = jnp.dot(unfolded, coeffs, precision=highest)
        image_summed = lax.psum(image_local, "col")
        gram_local = jnp.dot(image_summed.T, image_summed, precision=highest)
        gram = lax.psum(gram_local, "row")
        lower = jnp.linalg.cholesky(gram)
        factor = right_solve(lower, image_summed)
        coeffs = project(factor)
    core = coeffs.T
    return (factor * math.sqrt(I1), core)


def solution(mesh):
    return jax.shard_map(
        shards,
        mesh=mesh,
        in_specs=(P(None, "row", "col"), P("row", None), P("col", None), P()),
        out_specs=(P("row", None), P(None, "col")),
        check_vma=False,
    )
```

profile of v0, /device:TPU:2, one launch (start us, length us, event | category | flops | bytes accessed | tf_op | source)
XLA Modules:
  0.0 694.2 jit_solution(8862657409525127718)
XLA Ops:
  7.2 8.3 %fusion = f32[32,256,128]{2,0,1:T(8,128)S(1)} fusion(f32[32,32]{1,0:T(8,128)} %param.10, f32[4,8,256,128]{3,2,1,0:T(8,128)} %bitcast.65), kind=kOutput, calls=%fused_computation.1 | convolution fusion | flops 402653184 | bytes 8392704 | tf_op jit(solution)/shard_map/dot_general | solution.py:20
  15.6 5.0 convolution_bitcast_fusion
  20.6 4.7 copy.10
  25.3 112.8 %reduce-scatter.2.cloned.1.call-done = f32[256,32]{0,1:T(8,128)} async-done(((f32[256,1024]{0,1:T(8,128)}), f32[256,32]{0,1:T(8,128)}) %reduce-scatter.2.cloned.1.call-update) | async-done | bytes 32784 | tf_op jit(solution)/shard_map/reduce_scatter | solution.py:25
  138.1 0.9 fusion.13
  139.0 69.2 %psum.49 = f32[32,32]{1,0:T(8,128)S(1)} all-reduce(f32[32,32]{1,0:T(8,128)S(1)} %fusion.13), channel_id=1, replica_groups=mesh['row'=16,'col'=32] {'row'}, use_global_device_ids=true, to_apply=%region_1.0 | all-reduce | flops 1024 | bytes 8192 | tf_op jit(solution)/shard_map/psum | solution.py:29
  208.2 1.0 fusion.14
  209.2 90.0 %psum.50 = f32[256,32]{0,1:T(8,128)S(1)} all-reduce(f32[256,32]{0,1:T(8,128)S(1)} %fusion.14), channel_id=1, replica_groups=mesh['row'=16,'col'=32] {'col'}, use_global_device_ids=true, to_apply=%region_2.0 | all-reduce | flops 8192 | bytes 65536 | tf_op jit(solution)/shard_map/psum | solution.py:36
  299.4 71.7 %psum.51 = f32[32,32]{0,1:T(8,128)S(1)} all-reduce(f32[32,32]{0,1:T(8,128)S(1)} %fusion.15), channel_id=1, replica_groups=mesh['row'=16,'col'=32] {'row'}, use_global_device_ids=true, to_apply=%region_3.0 | all-reduce | flops 1024 | bytes 8192 | tf_op jit(solution)/shard_map/psum | solution.py:38
  371.1 2.9 cholesky.44
  374.1 0.6 compare_reduce_fusion.1
  374.7 0.7 fusion.3
  375.4 2.4 custom-call.6
  378.1 0.9 fusion.16
  379.0 69.5 %psum.52 = f32[32,32]{1,0:T(8,128)S(1)} all-reduce(f32[32,32]{1,0:T(8,128)S(1)} %fusion.16), channel_id=1, replica_groups=mesh['row'=16,'col'=32] {'row'}, use_global_device_ids=true, to_apply=%region_6.9 | all-reduce | flops 1024 | bytes 8192 | tf_op jit(solution)/shard_map/psum | solution.py:29
  448.5 1.0 fusion.17
  449.5 90.0 %psum.53 = f32[256,32]{0,1:T(8,128)S(1)} all-reduce(f32[256,32]{0,1:T(8,128)S(1)} %fusion.17), channel_id=1, replica_groups=mesh['row'=16,'col'=32] {'col'}, use_global_device_ids=true, to_apply=%region_7.10 | all-reduce | flops 8192 | bytes 65536 | tf_op jit(solution)/shard_map/psum | solution.py:36
  539.7 69.5 %psum.54 = f32[32,32]{0,1:T(8,128)S(1)} all-reduce(f32[32,32]{0,1:T(8,128)S(1)} %fusion.18), channel_id=1, replica_groups=mesh['row'=16,'col'=32] {'row'}, use_global_device_ids=true, to_apply=%region_8.11 | all-reduce | flops 1024 | bytes 8192 | tf_op jit(solution)/shard_map/psum | solution.py:38
  609.3 2.9 cholesky.55
  612.9 0.7 fusion.4
  613.6 2.4 custom-call.7
  616.0 0.9 broadcast_multiply_fusion
  616.9 0.9 fusion.19
  617.8 69.6 %psum.55 = f32[32,32]{1,0:T(8,128)} all-reduce(f32[32,32]{1,0:T(8,128)S(1)} %fusion.19), channel_id=1, replica_groups=mesh['row'=16,'col'=32] {'row'}, use_global_device_ids=true, to_apply=%region_9.12 | all-reduce | flops 1024 | bytes 8192 | tf_op jit(solution)/shard_map/psum | solution.py:29
  (16 shorter events, 1.5 us)
Async XLA Ops:
  7.2 130.9 %copy-start = (f32[256,32]{0,1:T(8,128)S(1)}, f32[256,32]{0,1:T(8,128)}, u32[]{:S(2)}) copy-start(f32[256,32]{0,1:T(8,128)} %param.8) | copy-start | bytes 98308
  7.2 130.9 %reduce-scatter.2.cloned.1.call-start = ((), (), s32[]{:S(2)}) async-start(), calls=%async_computation.1 | async-start | bytes 1081344 | tf_op jit(solution)/shard_map/reduce_scatter | solution.py:25
  7.2 8.3 %copy-start.1 = (f32[128,32]{0,1:T(8,128)S(1)}, f32[128,32]{0,1:T(8,128)}, u32[]{:S(2)}) copy-start(f32[128,32]{0,1:T(8,128)} %param.9) | copy-start | bytes 49156
Sparse Core Ops, SparseCore 0:
  25.4 112.5 reduce-scatter.1
where the time goes:
time: 695 us; the launch traced here: 694 us
  blocking collectives  530 us (76%)
  waiting for transfers between devices  113 us (16%)
  matrix products  19.4 us (3%)
  between operations  14.1 us (2%)
  other arithmetic  13.4 us (2%)
    psum x3, blocking collectives, project(): summed = lax.psum(local, 'row')  208 us
    psum x2, blocking collectives, shards(): image_summed = lax.psum(image_local, 'col')  180 us
    psum x2, blocking collectives, shards(): gram = lax.psum(gram_local, 'row')  141 us
    reduce_scatter x1, waiting for transfers between devices, shards(): lax.psum_scatter(partial_value, 'col', scatter_dimension=1, tiled=True)  113 us
  transfers between devices with their start and end apart: 1, of which 1 were waited for; matrix products, arithmetic and copies ran while one was open for 0% of the time, Pallas kernels for 0%

commit v1 on v0

v1 whole, which is shorter than its diff:
```python
import functools
import math

import jax
import jax.numpy as jnp
from jax import lax
from jax.experimental import pallas as pl
from jax.experimental.pallas import tpu as pltpu
from jax.sharding import PartitionSpec as P

I1 = 4096
RANK = 32
NEAR = 4
FAR = 4
ROWS = 256
COLS = 128
HIGHEST = lax.Precision.HIGHEST
F32 = jnp.float32
BF16 = jnp.bfloat16


def nn(a, b):
    return lax.dot_general(a, b, (((1,), (0,)), ((), ())), precision=HIGHEST, preferred_element_type=F32)


def nt(a, b):
    return lax.dot_general(a, b, (((1,), (1,)), ((), ())), precision=HIGHEST, preferred_element_type=F32)


def pack(square):
    return jnp.concatenate([square[8 * q : 8 * q + 8] for q in range(4)], axis=1)


def unpack(packed):
    return jnp.concatenate([packed[:, 32 * q : 32 * q + 32] for q in range(4)], axis=0)


def widen(packed):
    return jnp.concatenate([packed, jnp.zeros_like(packed)], axis=1)


def lower_solve(gram, sides):
    row_of = lax.broadcasted_iota(jnp.int32, (RANK, 1), 0)
    diagonal = jnp.zeros((RANK, 1), F32)
    for j in range(RANK):
        column = gram[:, j : j + 1]
        pivot = column[j : j + 1, :]
        diagonal = jnp.where(row_of == j, pivot, diagonal)
        factor = jnp.where(row_of > j, column, 0.0) / pivot
        sides = [side - factor * side[j : j + 1, :] for side in sides]
        gram = gram - factor * gram[j : j + 1, :]
    scale = lax.rsqrt(diagonal)
    return [side * scale for side in sides]


def contract_kernel(core_ref, factor_ref, tensor_ref, keep_ref, send_ref, left_ref, right_ref):
    depth = tensor_ref.shape[0]
    core = core_ref[0]
    place = lax.broadcasted_iota(jnp.int32, (RANK, RANK), 0)
    source = lax.broadcasted_iota(jnp.int32, (RANK, RANK), 1)
    half, near, far = place // 16, (place // FAR) % NEAR, place % FAR
    wanted = (far * NEAR + near) * 2 + (core + half) % 2
    chosen = nn((source == wanted).astype(F32), factor_ref[...])
    high = chosen.astype(BF16)
    low = (chosen - high.astype(F32)).astype(BF16)
    both = jnp.concatenate([high, low], axis=0)
    dims = (((1,), (1,)), ((), ()))
    for k in range(depth):
        piece = tensor_ref[k]
        piece_high = piece.astype(BF16)
        piece_low = (piece - piece_high.astype(F32)).astype(BF16)
        first = lax.dot_general(both, piece_high, dims, preferred_element_type=F32)
        second = lax.dot_general(high, piece_low, dims, preferred_element_type=F32)
        value = first[:RANK] + first[RANK:] + second
        at = pl.program_id(0) * depth + k
        left_ref[pl.ds(at, RANK, stride=RANK), :] = value[:, :128]
        right_ref[pl.ds(at, RANK, stride=RANK), :] = value[:, 128:]

    @pl.when(pl.program_id(0) == pl.num_programs(0) - 1)
    def _():
        for q, part_ref in enumerate((left_ref, right_ref)):
            keep_ref[:, 128 * q : 128 * q + 128] = part_ref[: 16 * RANK, :]
            send_ref[:, 128 * q : 128 * q + 128] = part_ref[16 * RANK :, :]


def contract(core, factor_two_t, tensor):
    depth = 4
    return pl.pallas_call(
        contract_kernel,
        grid=(RANK // depth,),
        in_specs=[
            pl.BlockSpec(memory_space=pltpu.SMEM),
            pl.BlockSpec((RANK, COLS), lambda g: (0, 0)),
            pl.BlockSpec((depth, ROWS, COLS), lambda g: (g, 0, 0)),
        ],
        out_specs=[pl.BlockSpec((16 * RANK, ROWS), lambda g: (0, 0))] * 2,
        out_shape=[jax.ShapeDtypeStruct((16 * RANK, ROWS), F32)] * 2,
        scratch_shapes=[pltpu.VMEM((RANK * RANK, 128), F32)] * 2,
        name="contract",
    )(core, factor_two_t, tensor)


def call(kernel, outs, *args):
    return pl.pallas_call(
        kernel,
        in_specs=[pl.BlockSpec(memory_space=pltpu.VMEM)] * len(args),
        out_specs=[pl.BlockSpec(memory_space=pltpu.VMEM)] * len(outs),
        out_shape=[jax.ShapeDtypeStruct(shape, F32) for shape in outs],
        name=kernel.__name__,
    )(*args)


def start_kernel(parts_ref, old_ref, own_ref, out_ref):
    own = jnp.sum(parts_ref[...], axis=0)
    own_ref[...] = own
    packed = pack(nt(old_ref[...], own))
    for q in range(16):
        out_ref[q] = packed


def weigh_kernel(parts_ref, three_ref, own_ref, out_ref):
    summed = unpack(jnp.sum(parts_ref[...], axis=0))
    three = three_ref[...]
    weighed = nt(nn(summed, three), three)
    payload = jnp.concatenate([own_ref[...], widen(pack(weighed))], axis=0)
    for q in range(FAR):
        out_ref[q] = payload


def block(mine_ref, other_ref):
    return jnp.concatenate(
        [mine_ref[:, :RANK, :].reshape(FAR * RANK, ROWS), other_ref[:, :RANK, :].reshape(FAR * RANK, ROWS)], axis=0
    )


def image_kernel(mine_ref, other_ref, out_ref):
    weights = jnp.concatenate(
        [unpack(ref[q, RANK : RANK + 8, :128]) for ref in (mine_ref, other_ref) for q in range(FAR)], axis=1
    )
    image = nn(weights, block(mine_ref, other_ref))
    for q in range(NEAR):
        out_ref[q] = image


def project_kernel(parts_ref, mine_ref, other_ref, out_ref):
    image = jnp.sum(parts_ref[...], axis=0)
    out = jnp.concatenate([nt(image, block(mine_ref, other_ref)), widen(pack(nt(image, image)))], axis=0)
    for q in range(16):
        out_ref[q] = out


def step_kernel(parts_ref, three_ref, mine_ref, other_ref, out_ref):
    summed = jnp.sum(parts_ref[...], axis=0)
    (coeffs,) = lower_solve(unpack(summed[RANK:, :128]), [summed[:RANK]])
    three = three_ref[...]
    mixing = nt(three, three)
    tiled = jnp.concatenate([jnp.concatenate([mixing] * 8, axis=0)] * 8, axis=1)
    left = lax.broadcasted_iota(jnp.int32, tiled.shape, 0) // RANK
    right = lax.broadcasted_iota(jnp.int32, tiled.shape, 1) // RANK
    weights = nn(coeffs, jnp.where(left == right, tiled, 0.0))
    image = nn(weights, block(mine_ref, other_ref))
    for q in range(NEAR):
        out_ref[q] = image


def last_kernel(parts_ref, own_ref, image_ref, out_ref):
    image = jnp.sum(parts_ref[...], axis=0)
    image_ref[...] = image
    out = jnp.concatenate([pack(nt(image, own_ref[...])), pack(nt(image, image))], axis=0)
    for q in range(16):
        out_ref[q] = out


def finish_kernel(parts_ref, image_ref, three_ref, factor_ref, core_ref):
    summed = jnp.sum(parts_ref[...], axis=0)
    factor, coeffs = lower_solve(unpack(summed[8:]), [image_ref[...], unpack(summed[:8])])
    factor_ref[...] = factor * math.sqrt(I1)
    core_ref[...] = nn(coeffs, three_ref[...])


def groups(of):
    found = {}
    for z in range(FAR * NEAR):
        for core in range(2):
            found.setdefault(of(z // NEAR, z % NEAR, core), []).append(z * 2 + core)
    return list(found.values())


NEAR_GROUPS = groups(lambda far, near, core: (far, core))
FAR_GROUPS = groups(lambda far, near, core: (near, core))
PAIRS = [(c, c ^ 1) for c in range(32)]


def exchange(values, axis, index_groups=None):
    return lax.all_to_all(values, axis, 0, 0, axis_index_groups=index_groups)


def shards(tensor, old_factor, factor_two, factor_three):
    core = (lax.axis_index("col") % 2).astype(jnp.int32).reshape(1)
    keep, send = contract(core, factor_two.T, tensor)
    partial_value = keep + lax.ppermute(send, "col", PAIRS)
    partial_value = exchange(partial_value.reshape(NEAR, FAR * RANK, ROWS), "col", NEAR_GROUPS)
    partial_value = jnp.sum(partial_value, axis=0).reshape(FAR, RANK, ROWS)
    parts = exchange(partial_value, "col", FAR_GROUPS)
    own, parts = call(start_kernel, [(RANK, ROWS), (16, 8, 128)], parts, old_factor.T)
    parts = exchange(parts, "row")
    (parts,) = call(weigh_kernel, [(FAR, RANK + 8, ROWS)], parts, factor_three, own)
    mine = exchange(parts, "col", FAR_GROUPS)
    other = lax.ppermute(mine, "col", PAIRS)
    (parts,) = call(image_kernel, [(NEAR, RANK, ROWS)], mine, other)
    parts = exchange(parts, "col", NEAR_GROUPS)
    (parts,) = call(project_kernel, [(16, RANK + 8, ROWS)], parts, mine, other)
    parts = exchange(parts, "row")
    (parts,) = call(step_kernel, [(NEAR, RANK, ROWS)], parts, factor_three, mine, other)
    parts = exchange(parts, "col", NEAR_GROUPS)
    image, parts = call(last_kernel, [(RANK, ROWS), (16, 16, 128)], parts, own)
    parts = exchange(parts, "row")
    factor, core_part = call(finish_kernel, [(RANK, ROWS), (RANK, RANK)], parts, image, factor_three)
    return factor.T, core_part


def solution(mesh):
    return jax.shard_map(
        shards,
        mesh=mesh,
        in_specs=(P(None, "row", "col"), P("row", None), P("col", None), P()),
        out_specs=(P("row", None), P(None, "col")),
        check_vma=False,
    )
```

time: 695 us -> 166 us (0.24)
  the two profiles are of different devices: /device:TPU:2 before, /device:TPU:32 now
where the time goes in v1:
time: 166 us; the launch traced here: 165 us
  blocking collectives  128 us (77%)
  Pallas kernels  27.1 us (16%)
  starting transfers between devices  3.82 us (2%)
  waiting for transfers between devices  3.45 us (2%)
    all_to_all x8, blocking collectives, exchange(): return lax.all_to_all(values, axis, 0, 0, axis_index_groups=index_groups)  128 us
    pallas_call x7, Pallas kernels, call(): pl.pallas_call(kernel, in_specs=[pl.BlockSpec(memory_space=pltpu.VMEM)] *...  19.5 us
    pallas_call x1, Pallas kernels, contract(): pl.pallas_call(contract_kernel, grid=(RANK // depth,), in_specs=[pl.Block...  7.62 us
  transfers between devices with their start and end apart: 2, of which 2 were waited for; matrix products, arithmetic and copies ran while one was open for 0% of the time, Pallas kernels for 0%

profile of v1, /device:TPU:32, one launch (start us, length us, event | category | flops | bytes accessed | tf_op | source)
XLA Modules:
  0.0 164.5 jit_solution(1272482660219887108)
XLA Ops:
  0.6 7.6 %contract.1 = (f32[512,256]{1,0:T(8,128)}, f32[512,256]{1,0:T(8,128)}) custom-call(s32[1]{0:T(128)} %bitcast.core_ref, f32[32,128]{1,0:T(8,128)} %bitcast.9, f32[32,256,128]{2,1,0:T(8,128)} %tensor_ref.1), custom_call_target="tpu_custom_call" | custom-call | tf_op jit(solution)/shard_map/contract/pallas_call | solution.py:88
  8.3 1.9 %collective-permute-start = (f32[512,256]{1,0:T(8,128)}, f32[512,256]{1,0:T(8,128)S(1)}, u32[]{:S(2)}, u32[]{:S(2)}) collective-permute-start(f32[512,256]{1,0:T(8,128)} %get-tuple-element.11), channel_id=1, source_target_pairs={{0,1},{1,0},{2,3},{3,2},{4,5},{5,4},{6,7},{7,6},{8,9},{9,8},{10,11... | collective-permute-start | bytes 1572872 | tf_op jit(solution)/shard_map/ppermute | solution.py:201
  10.2 2.1 %collective-permute-done = f32[512,256]{1,0:T(8,128)S(1)} collective-permute-done((f32[512,256]{1,0:T(8,128)}, f32[512,256]{1,0:T(8,128)S(1)}, u32[]{:S(2)}, u32[]{:S(2)}) %collective-permute-start) | collective-permute-done | bytes 524320 | tf_op jit(solution)/shard_map/ppermute | solution.py:201
  12.3 1.1 add.8
  13.4 21.1 %all_to_all.40 = f32[4,128,256]{2,1,0:T(8,128)S(1)} all-to-all(f32[4,128,256]{2,1,0:T(8,128)S(1)} %bitcast.6), channel_id=1, replica_groups={{0,2,4,6},{1,3,5,7},{8,10,12,14},{9,11,13,15},{16,18,20,22},{17,19,21,2..., dimensions={0} | all-to-all | bytes 1048576 | tf_op jit(solution)/shard_map/all_to_all | solution.py:195
  34.6 23.6 %all_to_all.41.parts_ref = f32[4,32,256]{2,1,0:T(8,128)} all-to-all(f32[4,32,256]{2,1,0:T(8,128)S(1)} %bitcast.7), channel_id=1, replica_groups={{0,8,16,24},{1,9,17,25},{2,10,18,26},{3,11,19,27},{4,12,20,28},{5,13,21..., dimensions={0} | all-to-all | bytes 262144 | tf_op jit(solution)/shard_map/all_to_all | solution.py:195
  58.1 1.8 %start_kernel.1 = (f32[32,256]{1,0:T(8,128)}, f32[16,8,128]{2,1,0:T(8,128)}) custom-call(f32[4,32,256]{2,1,0:T(8,128)} %all_to_all.41.parts_ref, f32[32,256]{1,0:T(8,128)} %bitcast.8), custom_call_target="tpu_custom_call" | custom-call | tf_op jit(solution)/shard_map/start_kernel/pallas_call | solution.py:104
  59.9 14.8 %all_to_all.42.parts_ref = f32[16,8,128]{2,1,0:T(8,128)} all-to-all(f32[16,8,128]{2,1,0:T(8,128)} %get-tuple-element.12), channel_id=1, replica_groups=mesh['row'=16,'col'=32] {'row'}, dimensions={0} | all-to-all | bytes 131072 | tf_op jit(solution)/shard_map/all_to_all | solution.py:195
  74.7 2.0 %weigh_kernel.1 = f32[4,40,256]{2,1,0:T(8,128)} custom-call(f32[16,8,128]{2,1,0:T(8,128)} %all_to_all.42.parts_ref, f32[32,32]{1,0:T(8,128)} %three_ref.5, f32[32,256]{1,0:T(8,128)} %get-tuple-element.13.own_ref), custom_call_target="tpu_custom_call" | custom-call | tf_op jit(solution)/shard_map/weigh_kernel/pallas_call | solution.py:104
  76.7 19.3 %all_to_all.43.mine_ref = f32[4,40,256]{2,1,0:T(8,128)S(1)} all-to-all(f32[4,40,256]{2,1,0:T(8,128)} %weigh_kernel.1), channel_id=1, replica_groups={{0,8,16,24},{1,9,17,25},{2,10,18,26},{3,11,19,27},{4,12,20,28},{5,13,21..., dimensions={0} | all-to-all | bytes 327680 | tf_op jit(solution)/shard_map/all_to_all | solution.py:195
  96.0 0.0 copy-start
  96.0 1.9 %collective-permute-start.1 = (f32[4,40,256]{2,1,0:T(8,128)S(1)}, f32[4,40,256]{2,1,0:T(8,128)S(1)}, u32[]{:S(2)}, u32[]{:S(2)}) collective-permute-start(f32[4,40,256]{2,1,0:T(8,128)S(1)} %all_to_all.43.mine_ref), channel_id=1, source_target_pairs={{0,1},{1,0},{2,3},{3,2},{4,5},{5,4},{6,7},{7,6},{8,9},{9,8},{10,11... | collective-permute-start | bytes 491528 | tf_op jit(solution)/shard_map/ppermute | solution.py:209
  97.9 1.4 collective-permute-done.1.other_ref
  99.2 0.0 copy-done
  99.3 0.7 copy-done.1
  99.9 2.0 %image_kernel.1 = f32[4,32,256]{2,1,0:T(8,128)} custom-call(f32[4,40,256]{2,1,0:T(8,128)} %copy-done, f32[4,40,256]{2,1,0:T(8,128)} %copy-done.1), custom_call_target="tpu_custom_call" | custom-call | tf_op jit(solution)/shard_map/image_kernel/pallas_call | solution.py:104
  101.9 10.2 %all_to_all.44.parts_ref = f32[4,32,256]{2,1,0:T(8,128)} all-to-all(f32[4,32,256]{2,1,0:T(8,128)} %image_kernel.1), channel_id=1, replica_groups={{0,2,4,6},{1,3,5,7},{8,10,12,14},{9,11,13,15},{16,18,20,22},{17,19,21,2..., dimensions={0} | all-to-all | bytes 262144 | tf_op jit(solution)/shard_map/all_to_all | solution.py:195
  112.1 2.3 %project_kernel.1 = f32[16,40,256]{2,1,0:T(8,128)} custom-call(f32[4,32,256]{2,1,0:T(8,128)} %all_to_all.44.parts_ref, f32[4,40,256]{2,1,0:T(8,128)} %copy-done, f32[4,40,256]{2,1,0:T(8,128)} %copy-done.1), custom_call_target="tpu_custom_call" | custom-call | tf_op jit(solution)/shard_map/project_kernel/pallas_call | solution.py:104
  114.4 16.6 %all_to_all.45.parts_ref = f32[16,40,256]{2,1,0:T(8,128)} all-to-all(f32[16,40,256]{2,1,0:T(8,128)} %project_kernel.1), channel_id=1, replica_groups=mesh['row'=16,'col'=32] {'row'}, dimensions={0} | all-to-all | bytes 1310720 | tf_op jit(solution)/shard_map/all_to_all | solution.py:195
  131.1 5.1 %step_kernel.1 = f32[4,32,256]{2,1,0:T(8,128)} custom-call(f32[16,40,256]{2,1,0:T(8,128)} %all_to_all.45.parts_ref, f32[32,32]{1,0:T(8,128)} %three_ref.5, f32[4,40,256]{2,1,0:T(8,128)} %copy-done, f32[4,40,256]{2,1,0:T(8,128)} %copy-done.1), custom_call_target="tpu_custom_call" | custom-call | tf_op jit(solution)/shard_map/step_kernel/pallas_call | solution.py:104
  136.2 9.9 %all_to_all.46.parts_ref = f32[4,32,256]{2,1,0:T(8,128)} all-to-all(f32[4,32,256]{2,1,0:T(8,128)} %step_kernel.1), channel_id=1, replica_groups={{0,2,4,6},{1,3,5,7},{8,10,12,14},{9,11,13,15},{16,18,20,22},{17,19,21,2..., dimensions={0} | all-to-all | bytes 262144 | tf_op jit(solution)/shard_map/all_to_all | solution.py:195
  146.1 1.8 %last_kernel.1 = (f32[32,256]{1,0:T(8,128)}, f32[16,16,128]{2,1,0:T(8,128)}) custom-call(f32[4,32,256]{2,1,0:T(8,128)} %all_to_all.46.parts_ref, f32[32,256]{1,0:T(8,128)} %get-tuple-element.13.own_ref), custom_call_target="tpu_custom_call" | custom-call | tf_op jit(solution)/shard_map/last_kernel/pallas_call | solution.py:104
  147.9 12.2 %all_to_all.47.parts_ref = f32[16,16,128]{2,1,0:T(8,128)} all-to-all(f32[16,16,128]{2,1,0:T(8,128)} %get-tuple-element.14), channel_id=1, replica_groups=mesh['row'=16,'col'=32] {'row'}, dimensions={0} | all-to-all | bytes 262144 | tf_op jit(solution)/shard_map/all_to_all | solution.py:195
  160.1 4.4 %finish_kernel.1 = (f32[32,256]{1,0:T(8,128)}, f32[32,32]{1,0:T(8,128)}) custom-call(f32[16,16,128]{2,1,0:T(8,128)} %all_to_all.47.parts_ref, f32[32,256]{1,0:T(8,128)} %get-tuple-element.15.image_ref, f32[32,32]{1,0:T(8,128)} %three_ref.5), custom_call_target="tpu_custom_call" | custom-call | tf_op jit(solution)/shard_map/finish_kernel/pallas_call | solution.py:104
  (2 shorter events, 0.0 us)
Async XLA Ops:
  8.3 4.0 %collective-permute-start = (f32[512,256]{1,0:T(8,128)}, f32[512,256]{1,0:T(8,128)S(1)}, u32[]{:S(2)}, u32[]{:S(2)}) collective-permute-start(f32[512,256]{1,0:T(8,128)} %get-tuple-element.11), channel_id=1, source_target_pairs={{0,1},{1,0},{2,3},{3,2},{4,5},{5,4},{6,7},{7,6},{8,9},{9,8},{10,11... | collective-permute-start | bytes 1572872 | tf_op jit(solution)/shard_map/ppermute | solution.py:201
  96.0 3.3 %copy-start = (f32[4,40,256]{2,1,0:T(8,128)}, f32[4,40,256]{2,1,0:T(8,128)S(1)}, u32[]{:S(2)}) copy-start(f32[4,40,256]{2,1,0:T(8,128)S(1)} %all_to_all.43.mine_ref) | copy-start | bytes 491524
  96.0 3.3 %collective-permute-start.1 = (f32[4,40,256]{2,1,0:T(8,128)S(1)}, f32[4,40,256]{2,1,0:T(8,128)S(1)}, u32[]{:S(2)}, u32[]{:S(2)}) collective-permute-start(f32[4,40,256]{2,1,0:T(8,128)S(1)} %all_to_all.43.mine_ref), channel_id=1, source_target_pairs={{0,1},{1,0},{2,3},{3,2},{4,5},{5,4},{6,7},{7,6},{8,9},{9,8},{10,11... | collective-permute-start | bytes 491528 | tf_op jit(solution)/shard_map/ppermute | solution.py:209
  99.3 0.7 copy-start.1

commit v2 on v1

v2 whole, which is shorter than its diff:
```python
import math

import jax
import jax.numpy as jnp
from jax import lax
from jax.experimental import pallas as pl
from jax.experimental.pallas import tpu as pltpu
from jax.sharding import PartitionSpec as P

I1 = 4096
RANK = 32
NEAR = 4
FAR = 4
GROUP = 2 * NEAR
ROWS = 256
COLS = 128
PANEL = 4
HIGHEST = lax.Precision.HIGHEST
F32 = jnp.float32
BF16 = jnp.bfloat16


def nn(a, b):
    return lax.dot_general(a, b, (((1,), (0,)), ((), ())), precision=HIGHEST, preferred_element_type=F32)


def nt(a, b):
    return lax.dot_general(a, b, (((1,), (1,)), ((), ())), precision=HIGHEST, preferred_element_type=F32)


def pack(square):
    return jnp.concatenate([square[8 * q : 8 * q + 8] for q in range(4)], axis=1)


def unpack(packed):
    return jnp.concatenate([packed[:, 32 * q : 32 * q + 32] for q in range(4)], axis=0)


def lower_solve(gram, sides):
    arrays = [jnp.concatenate([gram, jnp.zeros((RANK, 128 - RANK), F32)], axis=1), *sides]
    row_of = lax.broadcasted_iota(jnp.int32, (RANK, 128), 0)
    diagonal = jnp.zeros((RANK, 128), F32)
    for j in range(0, RANK, PANEL):
        columns = [jnp.broadcast_to(arrays[0][:, j + p : j + p + 1], (RANK, 128)) for p in range(PANEL)]
        factors = []
        for p in range(PANEL):
            pivot = columns[p][j + p : j + p + 1]
            diagonal = jnp.where(row_of == j + p, pivot, diagonal)
            factors.append(jnp.where(row_of > j + p, columns[p], 0.0) * (1.0 / pivot))
            for q in range(p + 1, PANEL):
                columns[q] = columns[q] - factors[p] * columns[q][j + p : j + p + 1]
        updated = []
        for array in arrays:
            rows = []
            for p in range(PANEL):
                row = array[j + p : j + p + 1]
                for q in range(p):
                    row = row - factors[q][j + p : j + p + 1] * rows[q]
                rows.append(row)
            for p in range(PANEL):
                array = array - factors[p] * rows[p]
            updated.append(array)
        arrays = updated
    scale = lax.rsqrt(diagonal)
    return [array * scale for array in arrays[1:]]


def contract_kernel(core_ref, factor_ref, tensor_ref, keep_ref, send_ref, left_ref, right_ref):
    depth = tensor_ref.shape[0]
    core = core_ref[0]
    place = lax.broadcasted_iota(jnp.int32, (RANK, RANK), 0)
    source = lax.broadcasted_iota(jnp.int32, (RANK, RANK), 1)
    half, near, far = place // 16, (place // FAR) % NEAR, place % FAR
    wanted = (far * NEAR + near) * 2 + (core + half) % 2
    chosen = nn((source == wanted).astype(F32), factor_ref[...])
    high = chosen.astype(BF16)
    low = (chosen - high.astype(F32)).astype(BF16)
    weights = jnp.concatenate([jnp.concatenate([part, part], axis=1) for part in (high, low)], axis=0)
    for k in range(depth):
        piece = tensor_ref[k]
        piece_high = piece.astype(BF16)
        piece_low = (piece - piece_high.astype(F32)).astype(BF16)
        pieces = jnp.concatenate([piece_high, piece_low], axis=1)
        both = lax.dot_general(weights, pieces, (((1,), (1,)), ((), ())), preferred_element_type=F32)
        value = both[:RANK] + both[RANK:]
        at = pl.program_id(0) * depth + k
        left_ref[pl.ds(at, RANK, stride=RANK), :] = value[:, :128]
        right_ref[pl.ds(at, RANK, stride=RANK), :] = value[:, 128:]

    @pl.when(pl.program_id(0) == pl.num_programs(0) - 1)
    def _():
        for q, part_ref in enumerate((left_ref, right_ref)):
            keep_ref[:, 128 * q : 128 * q + 128] = part_ref[: 16 * RANK, :]
            send_ref[:, 128 * q : 128 * q + 128] = part_ref[16 * RANK :, :]


def contract(core, factor_two_t, tensor):
    depth = 16
    return pl.pallas_call(
        contract_kernel,
        grid=(RANK // depth,),
        in_specs=[
            pl.BlockSpec(memory_space=pltpu.SMEM),
            pl.BlockSpec((RANK, COLS), lambda g: (0, 0)),
            pl.BlockSpec((depth, ROWS, COLS), lambda g: (g, 0, 0)),
        ],
        out_specs=[pl.BlockSpec(memory_space=pltpu.VMEM)] * 2,
        out_shape=[pltpu.VMEM((16 * RANK, ROWS), F32)] * 2,
        scratch_shapes=[pltpu.VMEM((RANK * RANK, 128), F32)] * 2,
        name="contract",
    )(core, factor_two_t, tensor)


def call(kernel, outs, *args, place=pltpu.VMEM):
    return pl.pallas_call(
        kernel,
        in_specs=[pl.BlockSpec(memory_space=pltpu.VMEM)] * len(args),
        out_specs=[pl.BlockSpec(memory_space=pltpu.VMEM)] * len(outs),
        out_shape=[place(shape, F32) for shape in outs],
        name=kernel.__name__,
    )(*[pltpu.with_memory_space_constraint(arg, pltpu.VMEM) for arg in args])


def start_kernel(parts_ref, old_ref, own_ref, out_ref):
    own = jnp.sum(parts_ref[...], axis=0)
    own_ref[...] = own
    packed = pack(nt(old_ref[...], own))
    for q in range(16):
        out_ref[q] = packed


def weigh_kernel(parts_ref, three_ref, own_ref, out_ref):
    summed = unpack(jnp.sum(parts_ref[...], axis=0))
    three = three_ref[...]
    packed = pack(nt(nn(summed, three), three))
    packed = jnp.concatenate([packed, jnp.zeros_like(packed)], axis=1)
    payload = jnp.concatenate([own_ref[...], packed], axis=0)
    for q in range(FAR):
        out_ref[q] = payload


def block(held_ref):
    return held_ref[:, :RANK, :].reshape(FAR * RANK, ROWS)


def image_kernel(held_ref, out_ref):
    weights = jnp.concatenate([unpack(held_ref[q, RANK : RANK + 8, :128]) for q in range(FAR)], axis=1)
    image = nn(weights, block(held_ref))
    for q in range(GROUP):
        out_ref[q] = image


def project_kernel(parts_ref, held_ref, out_ref):
    image = jnp.sum(parts_ref[...], axis=0)
    out = jnp.concatenate([nt(image, block(held_ref)), pack(nt(image, image))], axis=0)
    for q in range(16):
        out_ref[q] = out


def step_kernel(parts_ref, three_ref, held_ref, out_ref):
    summed = jnp.sum(parts_ref[...], axis=0)
    (coeffs,) = lower_solve(unpack(summed[RANK:]), [summed[:RANK]])
    three = three_ref[...]
    mixing = nt(three, three)
    tiled = jnp.concatenate([jnp.concatenate([mixing] * FAR, axis=0)] * FAR, axis=1)
    left = lax.broadcasted_iota(jnp.int32, tiled.shape, 0) // RANK
    right = lax.broadcasted_iota(jnp.int32, tiled.shape, 1) // RANK
    weights = nn(coeffs, jnp.where(left == right, tiled, 0.0))
    image = nn(weights, block(held_ref))
    for q in range(GROUP):
        out_ref[q] = image


def last_kernel(parts_ref, own_ref, image_ref, out_ref):
    image = jnp.sum(parts_ref[...], axis=0)
    image_ref[...] = image
    out = jnp.concatenate([pack(nt(image, own_ref[...])), pack(nt(image, image))], axis=0)
    for q in range(16):
        out_ref[q] = out


def finish_kernel(parts_ref, image_ref, three_ref, factor_ref, core_ref):
    summed = jnp.sum(parts_ref[...], axis=0)
    coeffs = jnp.concatenate([unpack(summed[:8]), jnp.zeros((RANK, 128 - RANK), F32)], axis=1)
    left, right, coeffs = lower_solve(unpack(summed[8:]), [image_ref[:, :128], image_ref[:, 128:], coeffs])
    factor_ref[:, :128] = left * math.sqrt(I1)
    factor_ref[:, 128:] = right * math.sqrt(I1)
    core_ref[...] = nn(coeffs[:, :RANK], three_ref[...])


def groups(of):
    found = {}
    for z in range(FAR * NEAR):
        for core in range(2):
            found.setdefault(of(z // NEAR, z % NEAR, core), []).append(z * 2 + core)
    return list(found.values())


NEAR_GROUPS = groups(lambda far, near, core: (far, core))
FAR_GROUPS = groups(lambda far, near, core: (near, core))
BLOCK_GROUPS = groups(lambda far, near, core: far)
PAIRS = [(c, c ^ 1) for c in range(32)]


def exchange(values, axis, index_groups=None):
    return lax.all_to_all(values, axis, 0, 0, axis_index_groups=index_groups)


def shards(tensor, old_factor, factor_two, factor_three):
    core = (lax.axis_index("col") & 1).astype(jnp.int32).reshape(1)
    keep, send = contract(core, factor_two.T, tensor)
    partial_value = keep + lax.ppermute(send, "col", PAIRS)
    partial_value = exchange(partial_value.reshape(NEAR, FAR * RANK, ROWS), "col", NEAR_GROUPS)
    partial_value = jnp.sum(partial_value, axis=0).reshape(FAR, RANK, ROWS)
    parts = exchange(partial_value, "col", FAR_GROUPS)
    own, parts = call(start_kernel, [(RANK, ROWS), (16, 8, 128)], parts, old_factor.T)
    parts = exchange(parts, "row")
    (parts,) = call(weigh_kernel, [(FAR, RANK + 8, ROWS)], parts, factor_three, own)
    held = exchange(parts, "col", FAR_GROUPS)
    (parts,) = call(image_kernel, [(GROUP, RANK, ROWS)], held)
    parts = exchange(parts, "col", BLOCK_GROUPS)
    (parts,) = call(project_kernel, [(16, RANK + 8, 128)], parts, held)
    parts = exchange(parts, "row")
    (parts,) = call(step_kernel, [(GROUP, RANK, ROWS)], parts, factor_three, held)
    parts = exchange(parts, "col", BLOCK_GROUPS)
    image, parts = call(last_kernel, [(RANK, ROWS), (16, 16, 128)], parts, own)
    parts = exchange(parts, "row")
    outs = [(RANK, ROWS), (RANK, RANK)]
    factor, core_part = call(finish_kernel, outs, parts, image, factor_three, place=jax.ShapeDtypeStruct)
    return factor.T, core_part


def solution(mesh):
    return jax.shard_map(
        shards,
        mesh=mesh,
        in_specs=(P(None, "row", "col"), P("row", None), P("col", None), P()),
        out_specs=(P("row", None), P(None, "col")),
        check_vma=False,
    )
```

time: 166 us -> 141 us (0.85)
  the two profiles are of different devices: /device:TPU:32 before, /device:TPU:2 now
where the time goes in v2:
time: 141 us; the launch traced here: 140 us
  blocking collectives  127 us (90%)
  Pallas kernels  8.8 us (6%)
  starting transfers between devices  1.92 us (1%)
  waiting for transfers between devices  1.88 us (1%)
    all_to_all x8, blocking collectives, exchange(): return lax.all_to_all(values, axis, 0, 0, axis_index_groups=index_groups)  127 us
    pallas_call x7, Pallas kernels, call(): pl.pallas_call(kernel, in_specs=[pl.BlockSpec(memory_space=pltpu.VMEM)] *...  5.2 us
    pallas_call x1, Pallas kernels, contract(): pl.pallas_call(contract_kernel, grid=(RANK // depth,), in_specs=[pl.Block...  3.6 us
  transfers between devices with their start and end apart: 1, of which 1 were waited for; matrix products, arithmetic and copies ran while one was open for 0% of the time, Pallas kernels for 0%

profile of v2, /device:TPU:2, one launch (start us, length us, event | category | flops | bytes accessed | tf_op | source)
XLA Modules:
  0.0 140.2 jit_solution(11979991244633748688)
XLA Ops:
  0.6 0.0 copy-start.1
  0.6 0.0 copy-start
  0.7 3.6 %contract.1 = (f32[512,256]{1,0:T(8,128)S(1)}, f32[512,256]{1,0:T(8,128)S(1)}) custom-call(s32[1]{0:T(128)} %bitcast.core_ref, f32[32,128]{1,0:T(8,128)} %bitcast.9, f32[32,256,128]{2,1,0:T(8,128)} %tensor_ref.1), custom_call_target="tpu_custom_call" | custom-call | tf_op jit(solution)/shard_map/contract/pallas_call | solution.py:99
  4.3 1.9 %collective-permute-start = (f32[512,256]{1,0:T(8,128)S(1)}, f32[512,256]{1,0:T(8,128)S(1)}, u32[]{:S(2)}, u32[]{:S(2)}) collective-permute-start(f32[512,256]{1,0:T(8,128)S(1)} %get-tuple-element.11), channel_id=1, source_target_pairs={{0,1},{1,0},{2,3},{3,2},{4,5},{5,4},{6,7},{7,6},{8,9},{9,8},{10,11... | collective-permute-start | bytes 1572872 | tf_op jit(solution)/shard_map/ppermute | solution.py:212
  6.2 1.9 %collective-permute-done = f32[512,256]{1,0:T(8,128)S(1)} collective-permute-done((f32[512,256]{1,0:T(8,128)S(1)}, f32[512,256]{1,0:T(8,128)S(1)}, u32[]{:S(2)}, u32[]{:S(2)}) %collective-permute-start) | collective-permute-done | bytes 524320 | tf_op jit(solution)/shard_map/ppermute | solution.py:212
  8.1 0.1 add.3
  8.1 20.5 %all_to_all.40 = f32[4,128,256]{2,1,0:T(8,128)S(1)} all-to-all(f32[4,128,256]{2,1,0:T(8,128)S(1)} %bitcast.7), channel_id=1, replica_groups={{0,2,4,6},{1,3,5,7},{8,10,12,14},{9,11,13,15},{16,18,20,22},{17,19,21,2..., dimensions={0} | all-to-all | bytes 1048576 | tf_op jit(solution)/shard_map/all_to_all | solution.py:206
  28.7 26.5 %all_to_all.41.parts_ref = f32[4,32,256]{2,1,0:T(8,128)S(1)} all-to-all(f32[4,32,256]{2,1,0:T(8,128)S(1)} %bitcast.8), channel_id=1, replica_groups={{0,8,16,24},{1,9,17,25},{2,10,18,26},{3,11,19,27},{4,12,20,28},{5,13,21..., dimensions={0} | all-to-all | bytes 262144 | tf_op jit(solution)/shard_map/all_to_all | solution.py:206
  55.2 0.0 copy-done.1
  55.2 0.2 start_kernel.1
  55.4 13.6 %all_to_all.42.parts_ref = f32[16,8,128]{2,1,0:T(8,128)S(1)} all-to-all(f32[16,8,128]{2,1,0:T(8,128)S(1)} %get-tuple-element.12), channel_id=1, replica_groups=mesh['row'=16,'col'=32] {'row'}, dimensions={0} | all-to-all | bytes 131072 | tf_op jit(solution)/shard_map/all_to_all | solution.py:206
  69.0 0.0 copy-done
  69.0 0.4 weigh_kernel.1
  69.4 17.5 %all_to_all.43.held_ref = f32[4,40,256]{2,1,0:T(8,128)S(1)} all-to-all(f32[4,40,256]{2,1,0:T(8,128)S(1)} %weigh_kernel.1), channel_id=1, replica_groups={{0,8,16,24},{1,9,17,25},{2,10,18,26},{3,11,19,27},{4,12,20,28},{5,13,21..., dimensions={0} | all-to-all | bytes 327680 | tf_op jit(solution)/shard_map/all_to_all | solution.py:206
  86.9 0.3 image_kernel.1
  87.2 13.1 %all_to_all.44.parts_ref = f32[8,32,256]{2,1,0:T(8,128)S(1)} all-to-all(f32[8,32,256]{2,1,0:T(8,128)S(1)} %image_kernel.1), channel_id=1, replica_groups={{0,1,2,3,4,5,6,7},{8,9,10,11,12,13,14,15},{16,17,18,19,20,21,22,23},{24..., dimensions={0} | all-to-all | bytes 524288 | tf_op jit(solution)/shard_map/all_to_all | solution.py:206
  100.3 0.3 project_kernel.1
  100.6 12.2 %all_to_all.45.parts_ref = f32[16,40,128]{2,1,0:T(8,128)S(1)} all-to-all(f32[16,40,128]{2,1,0:T(8,128)S(1)} %project_kernel.1), channel_id=1, replica_groups=mesh['row'=16,'col'=32] {'row'}, dimensions={0} | all-to-all | bytes 655360 | tf_op jit(solution)/shard_map/all_to_all | solution.py:206
  112.8 1.7 %step_kernel.1 = f32[8,32,256]{2,1,0:T(8,128)S(1)} custom-call(f32[16,40,128]{2,1,0:T(8,128)S(1)} %all_to_all.45.parts_ref, f32[32,32]{1,0:T(8,128)S(1)} %copy-done, f32[4,40,256]{2,1,0:T(8,128)S(1)} %all_to_all.43.held_ref), custom_call_target="tpu_custom_call" | custom-call | tf_op jit(solution)/shard_map/step_kernel/pallas_call | solution.py:115
  114.4 12.6 %all_to_all.46.parts_ref = f32[8,32,256]{2,1,0:T(8,128)S(1)} all-to-all(f32[8,32,256]{2,1,0:T(8,128)S(1)} %step_kernel.1), channel_id=1, replica_groups={{0,1,2,3,4,5,6,7},{8,9,10,11,12,13,14,15},{16,17,18,19,20,21,22,23},{24..., dimensions={0} | all-to-all | bytes 524288 | tf_op jit(solution)/shard_map/all_to_all | solution.py:206
  127.1 0.3 last_kernel.1
  127.4 10.9 %all_to_all.47.parts_ref = f32[16,16,128]{2,1,0:T(8,128)S(1)} all-to-all(f32[16,16,128]{2,1,0:T(8,128)S(1)} %get-tuple-element.14), channel_id=1, replica_groups=mesh['row'=16,'col'=32] {'row'}, dimensions={0} | all-to-all | bytes 262144 | tf_op jit(solution)/shard_map/all_to_all | solution.py:206
  138.2 2.0 %finish_kernel.1 = (f32[32,256]{1,0:T(8,128)}, f32[32,32]{1,0:T(8,128)}) custom-call(f32[16,16,128]{2,1,0:T(8,128)S(1)} %all_to_all.47.parts_ref, f32[32,256]{1,0:T(8,128)S(1)} %get-tuple-element.15.image_ref, f32[32,32]{1,0:T(8,128)S(1)} %copy-done), custom_call_target="tpu_custom_call" | custom-call | tf_op jit(solution)/shard_map/finish_kernel/pallas_call | solution.py:115
  (1 shorter events, 0.0 us)
Async XLA Ops:
  0.6 54.6 %copy-start.1 = (f32[256,32]{0,1:T(8,128)S(1)}, f32[256,32]{0,1:T(8,128)}, u32[]{:S(2)}) copy-start(f32[256,32]{0,1:T(8,128)} %param.5) | copy-start | bytes 98308
  0.6 68.4 %copy-start = (f32[32,32]{1,0:T(8,128)S(1)}, f32[32,32]{1,0:T(8,128)}, u32[]{:S(2)}) copy-start(f32[32,32]{1,0:T(8,128)} %three_ref.5) | copy-start | bytes 12292
  4.3 3.8 %collective-permute-start = (f32[512,256]{1,0:T(8,128)S(1)}, f32[512,256]{1,0:T(8,128)S(1)}, u32[]{:S(2)}, u32[]{:S(2)}) collective-permute-start(f32[512,256]{1,0:T(8,128)S(1)} %get-tuple-element.11), channel_id=1, source_target_pairs={{0,1},{1,0},{2,3},{3,2},{4,5},{5,4},{6,7},{7,6},{8,9},{9,8},{10,11... | collective-permute-start | bytes 1572872 | tf_op jit(solution)/shard_map/ppermute | solution.py:212

commit v3 on v2

v3 whole, which is shorter than its diff:
```python
import math

import jax
import jax.numpy as jnp
from jax import lax
from jax.experimental import pallas as pl
from jax.experimental.pallas import tpu as pltpu
from jax.sharding import PartitionSpec as P

I1 = 4096
RANK = 32
NEAR = 4
FAR = 4
PIECES = (8, 12, 12)
ROWS = 256
COLS = 128
PANEL = 8
HIGHEST = lax.Precision.HIGHEST
F32 = jnp.float32
BF16 = jnp.bfloat16


def nn(a, b):
    return lax.dot_general(a, b, (((1,), (0,)), ((), ())), precision=HIGHEST, preferred_element_type=F32)


def nt(a, b):
    return lax.dot_general(a, b, (((1,), (1,)), ((), ())), precision=HIGHEST, preferred_element_type=F32)


def pack(square):
    return jnp.concatenate([square[8 * q : 8 * q + 8] for q in range(4)], axis=1)


def unpack(packed):
    return jnp.concatenate([packed[:, 32 * q : 32 * q + 32] for q in range(4)], axis=0)


def lower_solve(gram, sides):
    arrays = [jnp.concatenate([gram, jnp.zeros((RANK, 128 - RANK), F32)], axis=1), *sides]
    row_of = lax.broadcasted_iota(jnp.int32, (RANK, 128), 0)
    diagonal = jnp.zeros((RANK, 128), F32)
    for j in range(0, RANK, PANEL):
        columns = [jnp.broadcast_to(arrays[0][:, j + p : j + p + 1], (RANK, 128)) for p in range(PANEL)]
        factors = []
        for p in range(PANEL):
            pivot = columns[p][j + p : j + p + 1]
            diagonal = jnp.where(row_of == j + p, pivot, diagonal)
            factors.append(jnp.where(row_of > j + p, columns[p], 0.0) * (1.0 / pivot))
            for q in range(p + 1, PANEL):
                columns[q] = columns[q] - factors[p] * columns[q][j + p : j + p + 1]
        updated = []
        for array in arrays:
            rows = []
            for p in range(PANEL):
                row = array[j + p : j + p + 1]
                for q in range(p):
                    row = row - factors[q][j + p : j + p + 1] * rows[q]
                rows.append(row)
            for p in range(PANEL):
                array = array - factors[p] * rows[p]
            updated.append(array)
        arrays = updated
    scale = lax.rsqrt(diagonal)
    return [array * scale for array in arrays[1:]]


def split(value):
    high = value.astype(BF16)
    return high, (value - high.astype(F32)).astype(BF16)


def contract_kernel(
    core_ref, factor_ref, tensor_ref, keep_ref, send_ref, left_ref, right_ref, two_ref, held_ref, arrived
):
    first = pltpu.make_async_copy(factor_ref, two_ref, arrived.at[len(PIECES)])
    first.start()
    starts = [sum(PIECES[:p]) for p in range(len(PIECES))]
    copies = [
        pltpu.make_async_copy(tensor_ref.at[pl.ds(start, size)], held_ref.at[pl.ds(start, size)], arrived.at[p])
        for p, (start, size) in enumerate(zip(starts, PIECES))
    ]
    for copy in copies:
        copy.start()
    place = lax.broadcasted_iota(jnp.int32, (RANK, RANK), 0)
    source = lax.broadcasted_iota(jnp.int32, (RANK, RANK), 1)
    near, far = (place // FAR) % NEAR, place % FAR
    core = (core_ref[0] + place // 16) % 2
    wanted = (far * NEAR + (near + far) % NEAR) * 2 + core
    first.wait()
    high, low = split(nn((source == wanted).astype(F32), two_ref[...]))
    weights = jnp.concatenate([jnp.concatenate([part, part], axis=1) for part in (high, low)], axis=0)
    for copy, start, size in zip(copies, starts, PIECES):
        copy.wait()
        for k in range(start, start + size):
            pieces = jnp.concatenate(split(held_ref[k]), axis=1)
            both = lax.dot_general(weights, pieces, (((1,), (1,)), ((), ())), preferred_element_type=F32)
            value = both[:RANK] + both[RANK:]
            left_ref[pl.ds(k, RANK, stride=RANK), :] = value[:, :128]
            right_ref[pl.ds(k, RANK, stride=RANK), :] = value[:, 128:]
    for q, part_ref in enumerate((left_ref, right_ref)):
        keep_ref[:, 128 * q : 128 * q + 128] = part_ref[: 16 * RANK, :]
        send_ref[:, 128 * q : 128 * q + 128] = part_ref[16 * RANK :, :]


def contract(core, factor_two_t, tensor):
    return pl.pallas_call(
        contract_kernel,
        in_specs=[
            pl.BlockSpec(memory_space=pltpu.SMEM),
            pl.BlockSpec(memory_space=pltpu.HBM),
            pl.BlockSpec(memory_space=pltpu.HBM),
        ],
        out_specs=[pl.BlockSpec(memory_space=pltpu.VMEM)] * 2,
        out_shape=[pltpu.VMEM((16 * RANK, ROWS), F32)] * 2,
        scratch_shapes=[
            pltpu.VMEM((RANK * RANK, 128), F32),
            pltpu.VMEM((RANK * RANK, 128), F32),
            pltpu.VMEM((RANK, COLS), F32),
            pltpu.VMEM((RANK, ROWS, COLS), F32),
            pltpu.SemaphoreType.DMA((len(PIECES) + 1,)),
        ],
        name="contract",
    )(core, factor_two_t, tensor)


def call(kernel, outs, *args, place=pltpu.VMEM):
    return pl.pallas_call(
        kernel,
        in_specs=[pl.BlockSpec(memory_space=pltpu.VMEM)] * len(args),
        out_specs=[pl.BlockSpec(memory_space=pltpu.VMEM)] * len(outs),
        out_shape=[place(shape, F32) for shape in outs],
        name=kernel.__name__,
    )(*[pltpu.with_memory_space_constraint(arg, pltpu.VMEM) for arg in args])


def total_kernel(parts_ref, out_ref):
    out_ref[...] = jnp.sum(parts_ref[...], axis=0)


def start_kernel(parts_ref, old_ref, own_ref, out_ref):
    own = jnp.sum(parts_ref[...], axis=0)
    own_ref[...] = own
    packed = pack(nt(old_ref[...], own))
    for q in range(16):
        out_ref[q] = packed


def weigh_kernel(parts_ref, three_ref, own_ref, out_ref):
    summed = unpack(jnp.sum(parts_ref[...], axis=0))
    three = three_ref[...]
    payload = jnp.concatenate([own_ref[:, :128], own_ref[:, 128:], pack(nt(nn(summed, three), three))], axis=0)
    for q in range(FAR):
        out_ref[q] = payload


def block(*held):
    rows = [jnp.concatenate([ref[q, :RANK], ref[q, RANK : 2 * RANK]], axis=1) for ref in held for q in range(FAR)]
    return jnp.concatenate(rows, axis=0)


def image_kernel(mine_ref, other_ref, out_ref):
    weights = [unpack(ref[q, 2 * RANK :]) for ref in (mine_ref, other_ref) for q in range(FAR)]
    image = nn(jnp.concatenate(weights, axis=1), block(mine_ref, other_ref))
    for q in range(NEAR):
        out_ref[q] = image


def project_kernel(parts_ref, mine_ref, other_ref, out_ref):
    image = jnp.sum(parts_ref[...], axis=0)
    projected = nt(image, block(mine_ref, other_ref))
    out = jnp.concatenate([projected[:, :128], projected[:, 128:], pack(nt(image, image))], axis=0)
    for q in range(16):
        out_ref[q] = out


def step_kernel(parts_ref, three_ref, mine_ref, other_ref, out_ref):
    summed = jnp.sum(parts_ref[...], axis=0)
    sides = lower_solve(unpack(summed[2 * RANK :]), [summed[:RANK], summed[RANK : 2 * RANK]])
    three = three_ref[...]
    mixing = nt(three, three)
    tiled = jnp.concatenate([jnp.concatenate([mixing] * FAR, axis=0)] * FAR, axis=1)
    left = lax.broadcasted_iota(jnp.int32, tiled.shape, 0) // RANK
    right = lax.broadcasted_iota(jnp.int32, tiled.shape, 1) // RANK
    mixing = jnp.where(left == right, tiled, 0.0)
    weights = jnp.concatenate([nn(side, mixing) for side in sides], axis=1)
    image = nn(weights, block(mine_ref, other_ref))
    for q in range(NEAR):
        out_ref[q] = image


def last_kernel(parts_ref, own_ref, image_ref, out_ref):
    image = jnp.sum(parts_ref[...], axis=0)
    image_ref[...] = image
    out = jnp.concatenate([pack(nt(image, own_ref[...])), pack(nt(image, image))], axis=0)
    for q in range(16):
        out_ref[q] = out


def finish_kernel(parts_ref, image_ref, three_ref, factor_ref, core_ref):
    summed = jnp.sum(parts_ref[...], axis=0)
    coeffs = jnp.concatenate([unpack(summed[:8]), jnp.zeros((RANK, 128 - RANK), F32)], axis=1)
    left, right, coeffs = lower_solve(unpack(summed[8:]), [image_ref[:, :128], image_ref[:, 128:], coeffs])
    factor_ref[:, :128] = left * math.sqrt(I1)
    factor_ref[:, 128:] = right * math.sqrt(I1)
    core_ref[...] = nn(coeffs[:, :RANK], three_ref[...])


def groups(by_far):
    found = [[] for _ in range(2 * FAR * NEAR // (FAR if by_far else NEAR))]
    for core in range(2):
        for far in range(FAR):
            for near in range(NEAR):
                chip = far * NEAR + (near + far) % NEAR
                found[(near if by_far else far) * 2 + core].append(chip * 2 + core)
    return found


NEAR_GROUPS = groups(by_far=False)
FAR_GROUPS = groups(by_far=True)
PAIRS = [(c, c ^ 1) for c in range(32)]


def exchange(values, axis, index_groups=None):
    return lax.all_to_all(values, axis, 0, 0, axis_index_groups=index_groups)


def shards(tensor, old_factor, factor_two, factor_three):
    core = (lax.axis_index("col") & 1).astype(jnp.int32).reshape(1)
    keep, send = contract(core, factor_two.T, tensor)
    value = keep + lax.ppermute(send, "col", PAIRS)
    parts = exchange(value.reshape(NEAR, FAR * RANK, ROWS), "col", NEAR_GROUPS)
    (value,) = call(total_kernel, [(FAR * RANK, ROWS)], parts)
    parts = exchange(value.reshape(FAR, RANK, ROWS), "col", FAR_GROUPS)
    own, parts = call(start_kernel, [(RANK, ROWS), (16, 8, 128)], parts, old_factor.T)
    parts = exchange(parts, "row")
    (parts,) = call(weigh_kernel, [(FAR, 2 * RANK + 8, 128)], parts, factor_three, own)
    mine = exchange(parts, "col", FAR_GROUPS)
    other = lax.ppermute(mine, "col", PAIRS)
    (parts,) = call(image_kernel, [(NEAR, RANK, ROWS)], mine, other)
    parts = exchange(parts, "col", NEAR_GROUPS)
    (parts,) = call(project_kernel, [(16, 2 * RANK + 8, 128)], parts, mine, other)
    parts = exchange(parts, "row")
    (parts,) = call(step_kernel, [(NEAR, RANK, ROWS)], parts, factor_three, mine, other)
    parts = exchange(parts, "col", NEAR_GROUPS)
    image, parts = call(last_kernel, [(RANK, ROWS), (16, 16, 128)], parts, own)
    parts = exchange(parts, "row")
    outs = [(RANK, ROWS), (RANK, RANK)]
    factor, core_part = call(finish_kernel, outs, parts, image, factor_three, place=jax.ShapeDtypeStruct)
    return factor.T, core_part


def solution(mesh):
    return jax.shard_map(
        shards,
        mesh=mesh,
        in_specs=(P(None, "row", "col"), P("row", None), P("col", None), P()),
        out_specs=(P("row", None), P(None, "col")),
        check_vma=False,
    )
```

time: 141 us -> 133 us (0.943)
  the two profiles are of different devices: /device:TPU:2 before, /device:TPU:32 now
where the time goes in v3:
time: 133 us; the launch traced here: 132 us
  blocking collectives  117 us (88%)
  Pallas kernels  7.74 us (6%)
  starting transfers between devices  3.83 us (3%)
  waiting for transfers between devices  3.21 us (2%)
    all_to_all x8, blocking collectives, exchange(): return lax.all_to_all(values, axis, 0, 0, axis_index_groups=index_groups)  117 us
    pallas_call x8, Pallas kernels, call(): pl.pallas_call(kernel, in_specs=[pl.BlockSpec(memory_space=pltpu.VMEM)] *...  4.51 us
    pallas_call x1, Pallas kernels, contract(): pl.pallas_call(contract_kernel, in_specs=[pl.BlockSpec(memory_space=pltpu...  3.23 us
  transfers between devices with their start and end apart: 2, of which 2 were waited for; matrix products, arithmetic and copies ran while one was open for 0% of the time, Pallas kernels for 0%

profile of v3, /device:TPU:32, one launch (start us, length us, event | category | flops | bytes accessed | tf_op | source)
XLA Modules:
  0.0 132.1 jit_solution(13901462050458949937)
XLA Ops:
  0.6 0.0 copy-start.1
  0.6 0.0 copy-start
  0.7 3.2 %contract.1 = (f32[512,256]{1,0:T(8,128)S(1)}, f32[512,256]{1,0:T(8,128)S(1)}) custom-call(s32[1]{0:T(128)} %bitcast.core_ref, f32[32,128]{1,0:T(8,128)} %bitcast.9, f32[32,256,128]{2,1,0:T(8,128)} %tensor_ref.1), custom_call_target="tpu_custom_call" | custom-call | tf_op jit(solution)/shard_map/contract/pallas_call | solution.py:107
  3.9 1.9 %collective-permute-start = (f32[512,256]{1,0:T(8,128)S(1)}, f32[512,256]{1,0:T(8,128)S(1)}, u32[]{:S(2)}, u32[]{:S(2)}) collective-permute-start(f32[512,256]{1,0:T(8,128)S(1)} %get-tuple-element.11), channel_id=1, source_target_pairs={{0,1},{1,0},{2,3},{3,2},{4,5},{5,4},{6,7},{7,6},{8,9},{9,8},{10,11... | collective-permute-start | bytes 1572872 | tf_op jit(solution)/shard_map/ppermute | solution.py:231
  5.8 1.9 %collective-permute-done = f32[512,256]{1,0:T(8,128)S(1)} collective-permute-done((f32[512,256]{1,0:T(8,128)S(1)}, f32[512,256]{1,0:T(8,128)S(1)}, u32[]{:S(2)}, u32[]{:S(2)}) %collective-permute-start) | collective-permute-done | bytes 524320 | tf_op jit(solution)/shard_map/ppermute | solution.py:231
  7.7 0.1 add.3
  7.8 21.1 %all_to_all.40.parts_ref = f32[4,128,256]{2,1,0:T(8,128)S(1)} all-to-all(f32[4,128,256]{2,1,0:T(8,128)S(1)} %bitcast.8), channel_id=1, replica_groups={{0,2,4,6},{1,3,5,7},{10,12,14,8},{11,13,15,9},{20,22,16,18},{21,23,17,1..., dimensions={0} | all-to-all | bytes 1048576 | tf_op jit(solution)/shard_map/all_to_all | solution.py:225
  28.9 22.1 %all_to_all.41.parts_ref = f32[4,32,256]{2,1,0:T(8,128)S(1)} all-to-all(f32[4,32,256]{2,1,0:T(8,128)S(1)} %bitcast.6), channel_id=1, replica_groups={{0,10,20,30},{1,11,21,31},{2,12,22,24},{3,13,23,25},{4,14,16,26},{5,15,..., dimensions={0} | all-to-all | bytes 262144 | tf_op jit(solution)/shard_map/all_to_all | solution.py:225
  51.0 0.0 copy-done.1
  51.0 0.2 start_kernel.1
  51.2 14.5 %all_to_all.42.parts_ref = f32[16,8,128]{2,1,0:T(8,128)S(1)} all-to-all(f32[16,8,128]{2,1,0:T(8,128)S(1)} %get-tuple-element.12), channel_id=1, replica_groups=mesh['row'=16,'col'=32] {'row'}, dimensions={0} | all-to-all | bytes 131072 | tf_op jit(solution)/shard_map/all_to_all | solution.py:225
  65.7 0.4 weigh_kernel.1
  66.2 15.0 %all_to_all.43.mine_ref = f32[4,72,128]{2,1,0:T(8,128)S(1)} all-to-all(f32[4,72,128]{2,1,0:T(8,128)S(1)} %weigh_kernel.1), channel_id=1, replica_groups={{0,10,20,30},{1,11,21,31},{2,12,22,24},{3,13,23,25},{4,14,16,26},{5,15,..., dimensions={0} | all-to-all | bytes 294912 | tf_op jit(solution)/shard_map/all_to_all | solution.py:225
  81.2 1.9 %collective-permute-start.1 = (f32[4,72,128]{2,1,0:T(8,128)S(1)}, f32[4,72,128]{2,1,0:T(8,128)S(1)}, u32[]{:S(2)}, u32[]{:S(2)}) collective-permute-start(f32[4,72,128]{2,1,0:T(8,128)S(1)} %all_to_all.43.mine_ref), channel_id=1, source_target_pairs={{0,1},{1,0},{2,3},{3,2},{4,5},{5,4},{6,7},{7,6},{8,9},{9,8},{10,11... | collective-permute-start | bytes 442376 | tf_op jit(solution)/shard_map/ppermute | solution.py:239
  83.1 1.3 %collective-permute-done.1.other_ref = f32[4,72,128]{2,1,0:T(8,128)S(1)} collective-permute-done((f32[4,72,128]{2,1,0:T(8,128)S(1)}, f32[4,72,128]{2,1,0:T(8,128)S(1)}, u32[]{:S(2)}, u32[]{:S(2)}) %collective-permute-start.1) | collective-permute-done | bytes 147488 | tf_op jit(solution)/shard_map/ppermute | solution.py:239
  84.4 0.3 image_kernel.1
  84.8 8.8 %all_to_all.44.parts_ref = f32[4,32,256]{2,1,0:T(8,128)S(1)} all-to-all(f32[4,32,256]{2,1,0:T(8,128)S(1)} %image_kernel.1), channel_id=1, replica_groups={{0,2,4,6},{1,3,5,7},{10,12,14,8},{11,13,15,9},{20,22,16,18},{21,23,17,1..., dimensions={0} | all-to-all | bytes 262144 | tf_op jit(solution)/shard_map/all_to_all | solution.py:225
  93.5 0.4 project_kernel.1
  94.0 14.3 %all_to_all.45.parts_ref = f32[16,72,128]{2,1,0:T(8,128)S(1)} all-to-all(f32[16,72,128]{2,1,0:T(8,128)S(1)} %project_kernel.1), channel_id=1, replica_groups=mesh['row'=16,'col'=32] {'row'}, dimensions={0} | all-to-all | bytes 1179648 | tf_op jit(solution)/shard_map/all_to_all | solution.py:225
  108.3 1.2 step_kernel.1
  109.5 9.6 %all_to_all.46.parts_ref = f32[4,32,256]{2,1,0:T(8,128)S(1)} all-to-all(f32[4,32,256]{2,1,0:T(8,128)S(1)} %step_kernel.1), channel_id=1, replica_groups={{0,2,4,6},{1,3,5,7},{10,12,14,8},{11,13,15,9},{20,22,16,18},{21,23,17,1..., dimensions={0} | all-to-all | bytes 262144 | tf_op jit(solution)/shard_map/all_to_all | solution.py:225
  119.1 0.3 last_kernel.1
  119.4 11.1 %all_to_all.47.parts_ref = f32[16,16,128]{2,1,0:T(8,128)S(1)} all-to-all(f32[16,16,128]{2,1,0:T(8,128)S(1)} %get-tuple-element.14), channel_id=1, replica_groups=mesh['row'=16,'col'=32] {'row'}, dimensions={0} | all-to-all | bytes 262144 | tf_op jit(solution)/shard_map/all_to_all | solution.py:225
  130.5 1.6 %finish_kernel.1 = (f32[32,256]{1,0:T(8,128)}, f32[32,32]{1,0:T(8,128)}) custom-call(f32[16,16,128]{2,1,0:T(8,128)S(1)} %all_to_all.47.parts_ref, f32[32,256]{1,0:T(8,128)S(1)} %get-tuple-element.15.image_ref, f32[32,32]{1,0:T(8,128)S(1)} %copy-done), custom_call_target="tpu_custom_call" | custom-call | tf_op jit(solution)/shard_map/finish_kernel/pallas_call | solution.py:128
  (2 shorter events, 0.0 us)
Async XLA Ops:
  0.6 50.4 %copy-start.1 = (f32[256,32]{0,1:T(8,128)S(1)}, f32[256,32]{0,1:T(8,128)}, u32[]{:S(2)}) copy-start(f32[256,32]{0,1:T(8,128)} %param.5) | copy-start | bytes 98308
  0.6 65.1 %copy-start = (f32[32,32]{1,0:T(8,128)S(1)}, f32[32,32]{1,0:T(8,128)}, u32[]{:S(2)}) copy-start(f32[32,32]{1,0:T(8,128)} %three_ref.5) | copy-start | bytes 12292
  3.9 3.8 %collective-permute-start = (f32[512,256]{1,0:T(8,128)S(1)}, f32[512,256]{1,0:T(8,128)S(1)}, u32[]{:S(2)}, u32[]{:S(2)}) collective-permute-start(f32[512,256]{1,0:T(8,128)S(1)} %get-tuple-element.11), channel_id=1, source_target_pairs={{0,1},{1,0},{2,3},{3,2},{4,5},{5,4},{6,7},{7,6},{8,9},{9,8},{10,11... | collective-permute-start | bytes 1572872 | tf_op jit(solution)/shard_map/ppermute | solution.py:231
  81.2 3.3 %collective-permute-start.1 = (f32[4,72,128]{2,1,0:T(8,128)S(1)}, f32[4,72,128]{2,1,0:T(8,128)S(1)}, u32[]{:S(2)}, u32[]{:S(2)}) collective-permute-start(f32[4,72,128]{2,1,0:T(8,128)S(1)} %all_to_all.43.mine_ref), channel_id=1, source_target_pairs={{0,1},{1,0},{2,3},{3,2},{4,5},{5,4},{6,7},{7,6},{8,9},{9,8},{10,11... | collective-permute-start | bytes 442376 | tf_op jit(solution)/shard_map/ppermute | solution.py:239

commit v4 on v3

--- a/solution.py
+++ b/solution.py
@@ -15,6 +15,7 @@
 ROWS = 256
 COLS = 128
 PANEL = 8
+SHIFT = 2
 HIGHEST = lax.Precision.HIGHEST
 F32 = jnp.float32
 BF16 = jnp.bfloat16
@@ -86,7 +87,7 @@
     source = lax.broadcasted_iota(jnp.int32, (RANK, RANK), 1)
     near, far = (place // FAR) % NEAR, place % FAR
     core = (core_ref[0] + place // 16) % 2
-    wanted = (far * NEAR + (near + far) % NEAR) * 2 + core
+    wanted = (far * NEAR + (near + far) % NEAR + SHIFT * core) % (FAR * NEAR) * 2 + core
     first.wait()
     high, low = split(nn((source == wanted).astype(F32), two_ref[...]))
     weights = jnp.concatenate([jnp.concatenate([part, part], axis=1) for part in (high, low)], axis=0)
@@ -154,37 +155,38 @@
         out_ref[q] = payload
 
 
-def block(*held):
-    rows = [jnp.concatenate([ref[q, :RANK], ref[q, RANK : 2 * RANK]], axis=1) for ref in held for q in range(FAR)]
+def block(held):
+    sides = [held[h, q] for h in range(2) for q in range(FAR)]
+    rows = [jnp.concatenate([side[:RANK], side[RANK : 2 * RANK]], axis=1) for side in sides]
     return jnp.concatenate(rows, axis=0)
 
 
-def image_kernel(mine_ref, other_ref, out_ref):
-    weights = [unpack(ref[q, 2 * RANK :]) for ref in (mine_ref, other_ref) for q in range(FAR)]
-    image = nn(jnp.concatenate(weights, axis=1), block(mine_ref, other_ref))
+def image_kernel(held_ref, out_ref):
+    weights = [unpack(held_ref[h, q, 2 * RANK :]) for h in range(2) for q in range(FAR)]
+    image = nn(jnp.concatenate(weights, axis=1), block(held_ref))
     for q in range(NEAR):
         out_ref[q] = image
 
 
-def project_kernel(parts_ref, mine_ref, other_ref, out_ref):
+def project_kernel(parts_ref, held_ref, out_ref):
     image = jnp.sum(parts_ref[...], axis=0)
-    projected = nt(image, block(mine_ref, other_ref))
+    projected = nt(image, block(held_ref))
     out = jnp.concatenate([projected[:, :128], projected[:, 128:], pack(nt(image, image))], axis=0)
     for q in range(16):
         out_ref[q] = out
 
 
-def step_kernel(parts_ref, three_ref, mine_ref, other_ref, out_ref):
+def step_kernel(parts_ref, three_ref, held_ref, out_ref):
     summed = jnp.sum(parts_ref[...], axis=0)
-    sides = lower_solve(unpack(summed[2 * RANK :]), [summed[:RANK], summed[RANK : 2 * RANK]])
     three = three_ref[...]
     mixing = nt(three, three)
     tiled = jnp.concatenate([jnp.concatenate([mixing] * FAR, axis=0)] * FAR, axis=1)
     left = lax.broadcasted_iota(jnp.int32, tiled.shape, 0) // RANK
     right = lax.broadcasted_iota(jnp.int32, tiled.shape, 1) // RANK
     mixing = jnp.where(left == right, tiled, 0.0)
-    weights = jnp.concatenate([nn(side, mixing) for side in sides], axis=1)
-    image = nn(weights, block(mine_ref, other_ref))
+    weights = [nt(summed[:RANK], mixing), nt(summed[RANK : 2 * RANK], mixing)]
+    sides = lower_solve(unpack(summed[2 * RANK :]), weights)
+    image = nn(jnp.concatenate(sides, axis=1), block(held_ref))
     for q in range(NEAR):
         out_ref[q] = image
 
@@ -199,25 +201,29 @@
 
 def finish_kernel(parts_ref, image_ref, three_ref, factor_ref, core_ref):
     summed = jnp.sum(parts_ref[...], axis=0)
-    coeffs = jnp.concatenate([unpack(summed[:8]), jnp.zeros((RANK, 128 - RANK), F32)], axis=1)
+    coeffs = nn(unpack(summed[:8]), three_ref[...])
+    coeffs = jnp.concatenate([coeffs, jnp.zeros((RANK, 128 - RANK), F32)], axis=1)
     left, right, coeffs = lower_solve(unpack(summed[8:]), [image_ref[:, :128], image_ref[:, 128:], coeffs])
     factor_ref[:, :128] = left * math.sqrt(I1)
     factor_ref[:, 128:] = right * math.sqrt(I1)
-    core_ref[...] = nn(coeffs[:, :RANK], three_ref[...])
-
-
-def groups(by_far):
+    core_ref[...] = coeffs[:, :RANK]
+
+
+def groups(by_far, shift=0):
     found = [[] for _ in range(2 * FAR * NEAR // (FAR if by_far else NEAR))]
     for core in range(2):
         for far in range(FAR):
             for near in range(NEAR):
-                chip = far * NEAR + (near + far) % NEAR
+                chip = (far * NEAR + (near + far) % NEAR + shift * core) % (FAR * NEAR)
                 found[(near if by_far else far) * 2 + core].append(chip * 2 + core)
     return found
 
 
 NEAR_GROUPS = groups(by_far=False)
 FAR_GROUPS = groups(by_far=True)
+NEAR_SCATTER = groups(by_far=False, shift=SHIFT)
+FAR_SCATTER = groups(by_far=True, shift=SHIFT)
+CORES = [[c, c + 1] for c in range(0, 32, 2)]
 PAIRS = [(c, c ^ 1) for c in range(32)]
 
 
@@ -229,19 +235,19 @@
     core = (lax.axis_index("col") & 1).astype(jnp.int32).reshape(1)
     keep, send = contract(core, factor_two.T, tensor)
     value = keep + lax.ppermute(send, "col", PAIRS)
-    parts = exchange(value.reshape(NEAR, FAR * RANK, ROWS), "col", NEAR_GROUPS)
+    parts = exchange(value.reshape(NEAR, FAR * RANK, ROWS), "col", NEAR_SCATTER)
     (value,) = call(total_kernel, [(FAR * RANK, ROWS)], parts)
-    parts = exchange(value.reshape(FAR, RANK, ROWS), "col", FAR_GROUPS)
+    parts = exchange(value.reshape(FAR, RANK, ROWS), "col", FAR_SCATTER)
     own, parts = call(start_kernel, [(RANK, ROWS), (16, 8, 128)], parts, old_factor.T)
     parts = exchange(parts, "row")
     (parts,) = call(weigh_kernel, [(FAR, 2 * RANK + 8, 128)], parts, factor_three, own)
     mine = exchange(parts, "col", FAR_GROUPS)
-    other = lax.ppermute(mine, "col", PAIRS)
-    (parts,) = call(image_kernel, [(NEAR, RANK, ROWS)], mine, other)
+    held = lax.all_gather(mine, "col", axis_index_groups=CORES)
+    (parts,) = call(image_kernel, [(NEAR, RANK, ROWS)], held)
     parts = exchange(parts, "col", NEAR_GROUPS)
-    (parts,) = call(project_kernel, [(16, 2 * RANK + 8, 128)], parts, mine, other)
+    (parts,) = call(project_kernel, [(16, 2 * RANK + 8, 128)], parts, held)
     parts = exchange(parts, "row")
-    (parts,) = call(step_kernel, [(NEAR, RANK, ROWS)], parts, factor_three, mine, other)
+    (parts,) = call(step_kernel, [(NEAR, RANK, ROWS)], parts, factor_three, held)
     parts = exchange(parts, "col", NEAR_GROUPS)
     image, parts = call(last_kernel, [(RANK, ROWS), (16, 16, 128)], parts, own)
     parts = exchange(parts, "row")

time: 133 us -> 130 us (0.977)
  starting transfers between devices: 3.83 us -> 1.92 us
  waiting for transfers between devices: 3.21 us -> 1.88 us
    all_gather x0 -> x1, blocking collectives: none -> 2 us  [shards(): held = lax.all_gather(mine, 'col', axis_index_groups=CORES)]
    ppermute x1 -> x0, starting transfers between devices: 1.91 us -> none  [shards(): other = lax.ppermute(mine, 'col', PAIRS)]
    ppermute x1 -> x0, waiting for transfers between devices: 1.34 us -> none  [shards(): other = lax.ppermute(mine, 'col', PAIRS)]
  transfers between devices with their start and end apart: 2 -> 1, of which waited for: 2 -> 1; matrix products, arithmetic and copies ran while one was open for 0% -> 0% of each run, Pallas kernels for 0% -> 0%
where the time goes in v4:
time: 130 us
  blocking collectives  118 us (91%)
  Pallas kernels  7.63 us (6%)
  starting transfers between devices  1.92 us (1%)
  waiting for transfers between devices  1.88 us (1%)
    all_to_all x8, blocking collectives, exchange(): return lax.all_to_all(values, axis, 0, 0, axis_index_groups=index_groups)  116 us
    pallas_call x8, Pallas kernels, call(): pl.pallas_call(kernel, in_specs=[pl.BlockSpec(memory_space=pltpu.VMEM)] *...  4.4 us
    pallas_call x1, Pallas kernels, contract(): pl.pallas_call(contract_kernel, in_specs=[pl.BlockSpec(memory_space=pltpu...  3.23 us
  transfers between devices with their start and end apart: 1, of which 1 were waited for; matrix products, arithmetic and copies ran while one was open for 0% of the time, Pallas kernels for 0%

profile of v4, /device:TPU:32, one launch (start us, length us, event | category | flops | bytes accessed | tf_op | source)
XLA Modules:
  0.0 130.1 jit_solution(14622906069987737436)
XLA Ops:
  0.6 0.0 copy-start.1
  0.6 0.0 copy-start
  0.7 3.2 %contract.1 = (f32[512,256]{1,0:T(8,128)S(1)}, f32[512,256]{1,0:T(8,128)S(1)}) custom-call(s32[1]{0:T(128)} %bitcast.core_ref, f32[32,128]{1,0:T(8,128)} %bitcast.13, f32[32,256,128]{2,1,0:T(8,128)} %tensor_ref.1), custom_call_target="tpu_custom_call" | custom-call | tf_op jit(solution)/shard_map/contract/pallas_call | solution.py:108
  3.9 1.9 %collective-permute-start = (f32[512,256]{1,0:T(8,128)S(1)}, f32[512,256]{1,0:T(8,128)S(1)}, u32[]{:S(2)}, u32[]{:S(2)}) collective-permute-start(f32[512,256]{1,0:T(8,128)S(1)} %get-tuple-element.11), channel_id=1, source_target_pairs={{0,1},{1,0},{2,3},{3,2},{4,5},{5,4},{6,7},{7,6},{8,9},{9,8},{10,11... | collective-permute-start | bytes 1572872 | tf_op jit(solution)/shard_map/ppermute | solution.py:237
  5.8 1.9 %collective-permute-done = f32[512,256]{1,0:T(8,128)S(1)} collective-permute-done((f32[512,256]{1,0:T(8,128)S(1)}, f32[512,256]{1,0:T(8,128)S(1)}, u32[]{:S(2)}, u32[]{:S(2)}) %collective-permute-start) | collective-permute-done | bytes 524320 | tf_op jit(solution)/shard_map/ppermute | solution.py:237
  7.7 0.1 add.3
  7.8 18.6 %all_to_all.40.parts_ref = f32[4,128,256]{2,1,0:T(8,128)S(1)} all-to-all(f32[4,128,256]{2,1,0:T(8,128)S(1)} %bitcast.12), channel_id=1, replica_groups={{0,2,4,6},{5,7,9,11},{10,12,14,8},{15,17,19,13},{20,22,16,18},{25,27,21..., dimensions={0} | all-to-all | bytes 1048576 | tf_op jit(solution)/shard_map/all_to_all | solution.py:231
  26.4 23.0 %all_to_all.41.parts_ref = f32[4,32,256]{2,1,0:T(8,128)S(1)} all-to-all(f32[4,32,256]{2,1,0:T(8,128)S(1)} %bitcast.10), channel_id=1, replica_groups={{0,10,20,30},{5,15,25,3},{2,12,22,24},{7,17,27,29},{4,14,16,26},{9,19,2..., dimensions={0} | all-to-all | bytes 262144 | tf_op jit(solution)/shard_map/all_to_all | solution.py:231
  49.4 0.0 copy-done.1
  49.4 0.2 start_kernel.1
  49.6 14.5 %all_to_all.42.parts_ref = f32[16,8,128]{2,1,0:T(8,128)S(1)} all-to-all(f32[16,8,128]{2,1,0:T(8,128)S(1)} %get-tuple-element.12), channel_id=1, replica_groups=mesh['row'=16,'col'=32] {'row'}, dimensions={0} | all-to-all | bytes 131072 | tf_op jit(solution)/shard_map/all_to_all | solution.py:231
  64.1 0.0 copy-done
  64.1 0.4 weigh_kernel.1
  64.6 16.5 %all_to_all.43 = f32[4,72,128]{2,1,0:T(8,128)S(1)} all-to-all(f32[4,72,128]{2,1,0:T(8,128)S(1)} %weigh_kernel.1), channel_id=1, replica_groups={{0,10,20,30},{1,11,21,31},{2,12,22,24},{3,13,23,25},{4,14,16,26},{5,15,..., dimensions={0} | all-to-all | bytes 294912 | tf_op jit(solution)/shard_map/all_to_all | solution.py:231
  81.1 2.0 %all-gather = f32[8,72,128]{2,1,0:T(8,128)S(1)} all-gather(f32[4,72,128]{2,1,0:T(8,128)S(1)} %all_to_all.43), channel_id=2, replica_groups={{0,1},{2,3},{4,5},{6,7},{8,9},{10,11},{12,13},{14,15},{16,17},{18,19},{..., dimensions={0}, use_global_device_ids=true | all-gather | bytes 442368 | tf_op jit(solution)/shard_map/all_gather | solution.py:245
  83.1 0.3 image_kernel.1
  83.4 8.3 %all_to_all.44.parts_ref = f32[4,32,256]{2,1,0:T(8,128)S(1)} all-to-all(f32[4,32,256]{2,1,0:T(8,128)S(1)} %image_kernel.1), channel_id=1, replica_groups={{0,2,4,6},{1,3,5,7},{10,12,14,8},{11,13,15,9},{20,22,16,18},{21,23,17,1..., dimensions={0} | all-to-all | bytes 262144 | tf_op jit(solution)/shard_map/all_to_all | solution.py:231
  91.6 0.4 project_kernel.1
  92.1 14.3 %all_to_all.45.parts_ref = f32[16,72,128]{2,1,0:T(8,128)S(1)} all-to-all(f32[16,72,128]{2,1,0:T(8,128)S(1)} %project_kernel.1), channel_id=1, replica_groups=mesh['row'=16,'col'=32] {'row'}, dimensions={0} | all-to-all | bytes 1179648 | tf_op jit(solution)/shard_map/all_to_all | solution.py:231
  106.4 1.3 step_kernel.1
  107.6 9.6 %all_to_all.46.parts_ref = f32[4,32,256]{2,1,0:T(8,128)S(1)} all-to-all(f32[4,32,256]{2,1,0:T(8,128)S(1)} %step_kernel.1), channel_id=1, replica_groups={{0,2,4,6},{1,3,5,7},{10,12,14,8},{11,13,15,9},{20,22,16,18},{21,23,17,1..., dimensions={0} | all-to-all | bytes 262144 | tf_op jit(solution)/shard_map/all_to_all | solution.py:231
  117.2 0.3 last_kernel.1
  117.5 11.1 %all_to_all.47.parts_ref = f32[16,16,128]{2,1,0:T(8,128)S(1)} all-to-all(f32[16,16,128]{2,1,0:T(8,128)S(1)} %get-tuple-element.14), channel_id=1, replica_groups=mesh['row'=16,'col'=32] {'row'}, dimensions={0} | all-to-all | bytes 262144 | tf_op jit(solution)/shard_map/all_to_all | solution.py:231
  128.6 1.4 %finish_kernel.1 = (f32[32,256]{1,0:T(8,128)}, f32[32,32]{1,0:T(8,128)}) custom-call(f32[16,16,128]{2,1,0:T(8,128)S(1)} %all_to_all.47.parts_ref, f32[32,256]{1,0:T(8,128)S(1)} %get-tuple-element.15.image_ref, f32[32,32]{1,0:T(8,128)S(1)} %copy-done), custom_call_target="tpu_custom_call" | custom-call | tf_op jit(solution)/shard_map/finish_kernel/pallas_call | solution.py:129
  (1 shorter events, 0.0 us)
Async XLA Ops:
  0.6 48.8 %copy-start.1 = (f32[256,32]{0,1:T(8,128)S(1)}, f32[256,32]{0,1:T(8,128)}, u32[]{:S(2)}) copy-start(f32[256,32]{0,1:T(8,128)} %param.5) | copy-start | bytes 98308
  0.6 63.5 %copy-start = (f32[32,32]{1,0:T(8,128)S(1)}, f32[32,32]{1,0:T(8,128)}, u32[]{:S(2)}) copy-start(f32[32,32]{1,0:T(8,128)} %three_ref.5) | copy-start | bytes 12292
  3.9 3.8 %collective-permute-start = (f32[512,256]{1,0:T(8,128)S(1)}, f32[512,256]{1,0:T(8,128)S(1)}, u32[]{:S(2)}, u32[]{:S(2)}) collective-permute-start(f32[512,256]{1,0:T(8,128)S(1)} %get-tuple-element.11), channel_id=1, source_target_pairs={{0,1},{1,0},{2,3},{3,2},{4,5},{5,4},{6,7},{7,6},{8,9},{9,8},{10,11... | collective-permute-start | bytes 1572872 | tf_op jit(solution)/shard_map/ppermute | solution.py:237

commit v5 on v4

--- a/solution.py
+++ b/solution.py
@@ -66,6 +66,15 @@
     return [array * scale for array in arrays[1:]]
 
 
+def swapped(index):
+    return index % 2 * 2 + index // 2
+
+
+def chip_of(near, far, core, shift):
+    near, far = swapped(near), swapped(far)
+    return (far * NEAR + (near + far * (1 + 2 * core)) % NEAR + shift * core) % (FAR * NEAR)
+
+
 def split(value):
     high = value.astype(BF16)
     return high, (value - high.astype(F32)).astype(BF16)
@@ -87,7 +96,7 @@
     source = lax.broadcasted_iota(jnp.int32, (RANK, RANK), 1)
     near, far = (place // FAR) % NEAR, place % FAR
     core = (core_ref[0] + place // 16) % 2
-    wanted = (far * NEAR + (near + far) % NEAR + SHIFT * core) % (FAR * NEAR) * 2 + core
+    wanted = chip_of(near, far, core, SHIFT) * 2 + core
     first.wait()
     high, low = split(nn((source == wanted).astype(F32), two_ref[...]))
     weights = jnp.concatenate([jnp.concatenate([part, part], axis=1) for part in (high, low)], axis=0)
@@ -214,7 +223,7 @@
     for core in range(2):
         for far in range(FAR):
             for near in range(NEAR):
-                chip = (far * NEAR + (near + far) % NEAR + shift * core) % (FAR * NEAR)
+                chip = chip_of(near, far, core, shift)
                 found[(near if by_far else far) * 2 + core].append(chip * 2 + core)
     return found
 
@@ -223,6 +232,7 @@
 FAR_GROUPS = groups(by_far=True)
 NEAR_SCATTER = groups(by_far=False, shift=SHIFT)
 FAR_SCATTER = groups(by_far=True, shift=SHIFT)
+ROW_GROUPS = [[10, 5, 0, 15, 6, 9, 12, 3, 2, 13, 8, 7, 14, 1, 4, 11]]
 CORES = [[c, c + 1] for c in range(0, 32, 2)]
 PAIRS = [(c, c ^ 1) for c in range(32)]
 
@@ -239,18 +249,18 @@
     (value,) = call(total_kernel, [(FAR * RANK, ROWS)], parts)
     parts = exchange(value.reshape(FAR, RANK, ROWS), "col", FAR_SCATTER)
     own, parts = call(start_kernel, [(RANK, ROWS), (16, 8, 128)], parts, old_factor.T)
-    parts = exchange(parts, "row")
+    parts = exchange(parts, "row", ROW_GROUPS)
     (parts,) = call(weigh_kernel, [(FAR, 2 * RANK + 8, 128)], parts, factor_three, own)
     mine = exchange(parts, "col", FAR_GROUPS)
     held = lax.all_gather(mine, "col", axis_index_groups=CORES)
     (parts,) = call(image_kernel, [(NEAR, RANK, ROWS)], held)
     parts = exchange(parts, "col", NEAR_GROUPS)
     (parts,) = call(project_kernel, [(16, 2 * RANK + 8, 128)], parts, held)
-    parts = exchange(parts, "row")
+    parts = exchange(parts, "row", ROW_GROUPS)
     (parts,) = call(step_kernel, [(NEAR, RANK, ROWS)], parts, factor_three, held)
     parts = exchange(parts, "col", NEAR_GROUPS)
     image, parts = call(last_kernel, [(RANK, ROWS), (16, 16, 128)], parts, own)
-    parts = exchange(parts, "row")
+    parts = exchange(parts, "row", ROW_GROUPS)
     outs = [(RANK, ROWS), (RANK, RANK)]
     factor, core_part = call(finish_kernel, outs, parts, image, factor_three, place=jax.ShapeDtypeStruct)
     return factor.T, core_part

time: 130 us -> 126 us (0.969)
  the two profiles are of different devices: /device:TPU:32 before, /device:TPU:4 now
where the time goes in v5:
time: 126 us; the launch traced here: 125 us
  blocking collectives  113 us (90%)
  Pallas kernels  7.63 us (6%)
  starting transfers between devices  1.92 us (2%)
  waiting for transfers between devices  1.88 us (1%)
    all_to_all x8, blocking collectives, exchange(): return lax.all_to_all(values, axis, 0, 0, axis_index_groups=index_groups)  111 us
    pallas_call x8, Pallas kernels, call(): pl.pallas_call(kernel, in_specs=[pl.BlockSpec(memory_space=pltpu.VMEM)] *...  4.4 us
    pallas_call x1, Pallas kernels, contract(): pl.pallas_call(contract_kernel, in_specs=[pl.BlockSpec(memory_space=pltpu...  3.23 us
  transfers between devices with their start and end apart: 1, of which 1 were waited for; matrix products, arithmetic and copies ran while one was open for 0% of the time, Pallas kernels for 0%

profile of v5, /device:TPU:4, one launch (start us, length us, event | category | flops | bytes accessed | tf_op | source)
XLA Modules:
  0.0 125.3 jit_solution(15272353346663053278)
XLA Ops:
  0.6 0.0 copy-start.1
  0.6 0.0 copy-start
  0.7 3.2 %contract.1 = (f32[512,256]{1,0:T(8,128)S(1)}, f32[512,256]{1,0:T(8,128)S(1)}) custom-call(s32[1]{0:T(128)} %bitcast.core_ref, f32[32,128]{1,0:T(8,128)} %bitcast.13, f32[32,256,128]{2,1,0:T(8,128)} %tensor_ref.1), custom_call_target="tpu_custom_call" | custom-call | tf_op jit(solution)/shard_map/contract/pallas_call | solution.py:117
  3.9 1.9 %collective-permute-start = (f32[512,256]{1,0:T(8,128)S(1)}, f32[512,256]{1,0:T(8,128)S(1)}, u32[]{:S(2)}, u32[]{:S(2)}) collective-permute-start(f32[512,256]{1,0:T(8,128)S(1)} %get-tuple-element.11), channel_id=1, source_target_pairs={{0,1},{1,0},{2,3},{3,2},{4,5},{5,4},{6,7},{7,6},{8,9},{9,8},{10,11... | collective-permute-start | bytes 1572872 | tf_op jit(solution)/shard_map/ppermute | solution.py:247
  5.8 1.9 %collective-permute-done = f32[512,256]{1,0:T(8,128)S(1)} collective-permute-done((f32[512,256]{1,0:T(8,128)S(1)}, f32[512,256]{1,0:T(8,128)S(1)}, u32[]{:S(2)}, u32[]{:S(2)}) %collective-permute-start) | collective-permute-done | bytes 524320 | tf_op jit(solution)/shard_map/ppermute | solution.py:247
  7.7 0.1 add.3
  7.8 18.0 %all_to_all.40.parts_ref = f32[4,128,256]{2,1,0:T(8,128)S(1)} all-to-all(f32[4,128,256]{2,1,0:T(8,128)S(1)} %bitcast.12), channel_id=1, replica_groups={{0,4,2,6},{5,9,7,11},{20,16,22,18},{25,21,27,23},{10,14,12,8},{19,15,13..., dimensions={0} | all-to-all | bytes 1048576 | tf_op jit(solution)/shard_map/all_to_all | solution.py:241
  25.8 22.8 %all_to_all.41.parts_ref = f32[4,32,256]{2,1,0:T(8,128)S(1)} all-to-all(f32[4,32,256]{2,1,0:T(8,128)S(1)} %bitcast.10), channel_id=1, replica_groups={{0,20,10,30},{5,25,19,31},{4,16,14,26},{9,21,15,3},{2,22,12,24},{7,27,1..., dimensions={0} | all-to-all | bytes 262144 | tf_op jit(solution)/shard_map/all_to_all | solution.py:241
  48.6 0.0 copy-done.1
  48.6 0.2 start_kernel.1
  48.8 11.3 %all_to_all.42.parts_ref = f32[16,8,128]{2,1,0:T(8,128)S(1)} all-to-all(f32[16,8,128]{2,1,0:T(8,128)S(1)} %get-tuple-element.12), channel_id=1, replica_groups={{320,160,0,480,192,288,384,96,64,416,256,224,448,32,128,352},{321,161,1..., dimensions={0} | all-to-all | bytes 131072 | tf_op jit(solution)/shard_map/all_to_all | solution.py:241
  60.1 0.0 copy-done
  60.1 0.4 weigh_kernel.1
  60.5 16.5 %all_to_all.43 = f32[4,72,128]{2,1,0:T(8,128)S(1)} all-to-all(f32[4,72,128]{2,1,0:T(8,128)S(1)} %weigh_kernel.1), channel_id=1, replica_groups={{0,20,10,30},{1,21,15,27},{4,16,14,26},{5,17,11,31},{2,22,12,24},{3,23,..., dimensions={0} | all-to-all | bytes 294912 | tf_op jit(solution)/shard_map/all_to_all | solution.py:241
  77.0 2.0 %all-gather = f32[8,72,128]{2,1,0:T(8,128)S(1)} all-gather(f32[4,72,128]{2,1,0:T(8,128)S(1)} %all_to_all.43), channel_id=2, replica_groups={{0,1},{2,3},{4,5},{6,7},{8,9},{10,11},{12,13},{14,15},{16,17},{18,19},{..., dimensions={0}, use_global_device_ids=true | all-gather | bytes 442368 | tf_op jit(solution)/shard_map/all_gather | solution.py:255
  79.0 0.3 image_kernel.1
  79.3 9.6 %all_to_all.44.parts_ref = f32[4,32,256]{2,1,0:T(8,128)S(1)} all-to-all(f32[4,32,256]{2,1,0:T(8,128)S(1)} %image_kernel.1), channel_id=1, replica_groups={{0,4,2,6},{1,5,3,7},{20,16,22,18},{21,17,23,19},{10,14,12,8},{15,11,9,1..., dimensions={0} | all-to-all | bytes 262144 | tf_op jit(solution)/shard_map/all_to_all | solution.py:241
  89.0 0.4 project_kernel.1
  89.4 13.7 %all_to_all.45.parts_ref = f32[16,72,128]{2,1,0:T(8,128)S(1)} all-to-all(f32[16,72,128]{2,1,0:T(8,128)S(1)} %project_kernel.1), channel_id=1, replica_groups={{320,160,0,480,192,288,384,96,64,416,256,224,448,32,128,352},{321,161,1..., dimensions={0} | all-to-all | bytes 1179648 | tf_op jit(solution)/shard_map/all_to_all | solution.py:241
  103.2 1.3 %step_kernel.1 = f32[4,32,256]{2,1,0:T(8,128)S(1)} custom-call(f32[16,72,128]{2,1,0:T(8,128)S(1)} %all_to_all.45.parts_ref, f32[32,32]{1,0:T(8,128)S(1)} %copy-done, f32[2,4,72,128]{3,2,1,0:T(8,128)S(1)} %bitcast.9), custom_call_target="tpu_custom_call" | custom-call | tf_op jit(solution)/shard_map/step_kernel/pallas_call | solution.py:138
  104.4 8.6 %all_to_all.46.parts_ref = f32[4,32,256]{2,1,0:T(8,128)S(1)} all-to-all(f32[4,32,256]{2,1,0:T(8,128)S(1)} %step_kernel.1), channel_id=1, replica_groups={{0,4,2,6},{1,5,3,7},{20,16,22,18},{21,17,23,19},{10,14,12,8},{15,11,9,1..., dimensions={0} | all-to-all | bytes 262144 | tf_op jit(solution)/shard_map/all_to_all | solution.py:241
  113.0 0.3 last_kernel.1
  113.3 10.6 %all_to_all.47.parts_ref = f32[16,16,128]{2,1,0:T(8,128)S(1)} all-to-all(f32[16,16,128]{2,1,0:T(8,128)S(1)} %get-tuple-element.14), channel_id=1, replica_groups={{320,160,0,480,192,288,384,96,64,416,256,224,448,32,128,352},{321,161,1..., dimensions={0} | all-to-all | bytes 262144 | tf_op jit(solution)/shard_map/all_to_all | solution.py:241
  123.9 1.4 %finish_kernel.1 = (f32[32,256]{1,0:T(8,128)}, f32[32,32]{1,0:T(8,128)}) custom-call(f32[16,16,128]{2,1,0:T(8,128)S(1)} %all_to_all.47.parts_ref, f32[32,256]{1,0:T(8,128)S(1)} %get-tuple-element.15.image_ref, f32[32,32]{1,0:T(8,128)S(1)} %copy-done), custom_call_target="tpu_custom_call" | custom-call | tf_op jit(solution)/shard_map/finish_kernel/pallas_call | solution.py:138
  (1 shorter events, 0.0 us)
Async XLA Ops:
  0.6 48.0 %copy-start.1 = (f32[256,32]{0,1:T(8,128)S(1)}, f32[256,32]{0,1:T(8,128)}, u32[]{:S(2)}) copy-start(f32[256,32]{0,1:T(8,128)} %param.5) | copy-start | bytes 98308
  0.6 59.5 %copy-start = (f32[32,32]{1,0:T(8,128)S(1)}, f32[32,32]{1,0:T(8,128)}, u32[]{:S(2)}) copy-start(f32[32,32]{1,0:T(8,128)} %three_ref.5) | copy-start | bytes 12292
  3.9 3.8 %collective-permute-start = (f32[512,256]{1,0:T(8,128)S(1)}, f32[512,256]{1,0:T(8,128)S(1)}, u32[]{:S(2)}, u32[]{:S(2)}) collective-permute-start(f32[512,256]{1,0:T(8,128)S(1)} %get-tuple-element.11), channel_id=1, source_target_pairs={{0,1},{1,0},{2,3},{3,2},{4,5},{5,4},{6,7},{7,6},{8,9},{9,8},{10,11... | collective-permute-start | bytes 1572872 | tf_op jit(solution)/shard_map/ppermute | solution.py:247

commit v6 on v5

--- a/solution.py
+++ b/solution.py
@@ -230,6 +230,8 @@
 
 NEAR_GROUPS = groups(by_far=False)
 FAR_GROUPS = groups(by_far=True)
+NEAR_GATHER = [group[:: 1 - 2 * (group[0] % 2)] for group in NEAR_GROUPS]
+FAR_GATHER = [group[:: 1 - 2 * (group[0] % 2)] for group in FAR_GROUPS]
 NEAR_SCATTER = groups(by_far=False, shift=SHIFT)
 FAR_SCATTER = groups(by_far=True, shift=SHIFT)
 ROW_GROUPS = [[10, 5, 0, 15, 6, 9, 12, 3, 2, 13, 8, 7, 14, 1, 4, 11]]
@@ -251,14 +253,14 @@
     own, parts = call(start_kernel, [(RANK, ROWS), (16, 8, 128)], parts, old_factor.T)
     parts = exchange(parts, "row", ROW_GROUPS)
     (parts,) = call(weigh_kernel, [(FAR, 2 * RANK + 8, 128)], parts, factor_three, own)
-    mine = exchange(parts, "col", FAR_GROUPS)
+    mine = exchange(parts, "col", FAR_GATHER)
     held = lax.all_gather(mine, "col", axis_index_groups=CORES)
     (parts,) = call(image_kernel, [(NEAR, RANK, ROWS)], held)
-    parts = exchange(parts, "col", NEAR_GROUPS)
+    parts = exchange(parts, "col", NEAR_GATHER)
     (parts,) = call(project_kernel, [(16, 2 * RANK + 8, 128)], parts, held)
     parts = exchange(parts, "row", ROW_GROUPS)
     (parts,) = call(step_kernel, [(NEAR, RANK, ROWS)], parts, factor_three, held)
-    parts = exchange(parts, "col", NEAR_GROUPS)
+    parts = exchange(parts, "col", NEAR_GATHER)
     image, parts = call(last_kernel, [(RANK, ROWS), (16, 16, 128)], parts, own)
     parts = exchange(parts, "row", ROW_GROUPS)
     outs = [(RANK, ROWS), (RANK, RANK)]

time: 126 us -> 127 us (level)
  no operation moved by 1% of the time
where the time goes in v6:
time: 127 us; the launch traced here: 126 us
  blocking collectives  114 us (90%)
  Pallas kernels  7.63 us (6%)
  starting transfers between devices  1.92 us (2%)
  waiting for transfers between devices  1.88 us (1%)
    all_to_all x8, blocking collectives, exchange(): return lax.all_to_all(values, axis, 0, 0, axis_index_groups=index_groups)  112 us
    pallas_call x8, Pallas kernels, call(): pl.pallas_call(kernel, in_specs=[pl.BlockSpec(memory_space=pltpu.VMEM)] *...  4.4 us
    pallas_call x1, Pallas kernels, contract(): pl.pallas_call(contract_kernel, in_specs=[pl.BlockSpec(memory_space=pltpu...  3.23 us
  transfers between devices with their start and end apart: 1, of which 1 were waited for; matrix products, arithmetic and copies ran while one was open for 0% of the time, Pallas kernels for 0%

profile of v6, /device:TPU:4, one launch (start us, length us, event | category | flops | bytes accessed | tf_op | source)
XLA Modules:
  0.0 126.3 jit_solution(2621228546824269618)
XLA Ops:
  0.6 0.0 copy-start.1
  0.6 0.0 copy-start
  0.7 3.2 %contract.1 = (f32[512,256]{1,0:T(8,128)S(1)}, f32[512,256]{1,0:T(8,128)S(1)}) custom-call(s32[1]{0:T(128)} %bitcast.core_ref, f32[32,128]{1,0:T(8,128)} %bitcast.13, f32[32,256,128]{2,1,0:T(8,128)} %tensor_ref.1), custom_call_target="tpu_custom_call" | custom-call | tf_op jit(solution)/shard_map/contract/pallas_call | solution.py:117
  3.9 1.9 %collective-permute-start = (f32[512,256]{1,0:T(8,128)S(1)}, f32[512,256]{1,0:T(8,128)S(1)}, u32[]{:S(2)}, u32[]{:S(2)}) collective-permute-start(f32[512,256]{1,0:T(8,128)S(1)} %get-tuple-element.11), channel_id=1, source_target_pairs={{0,1},{1,0},{2,3},{3,2},{4,5},{5,4},{6,7},{7,6},{8,9},{9,8},{10,11... | collective-permute-start | bytes 1572872 | tf_op jit(solution)/shard_map/ppermute | solution.py:249
  5.8 1.9 %collective-permute-done = f32[512,256]{1,0:T(8,128)S(1)} collective-permute-done((f32[512,256]{1,0:T(8,128)S(1)}, f32[512,256]{1,0:T(8,128)S(1)}, u32[]{:S(2)}, u32[]{:S(2)}) %collective-permute-start) | collective-permute-done | bytes 524320 | tf_op jit(solution)/shard_map/ppermute | solution.py:249
  7.7 0.1 add.3
  7.8 18.0 %all_to_all.40.parts_ref = f32[4,128,256]{2,1,0:T(8,128)S(1)} all-to-all(f32[4,128,256]{2,1,0:T(8,128)S(1)} %bitcast.12), channel_id=1, replica_groups={{0,4,2,6},{5,9,7,11},{20,16,22,18},{25,21,27,23},{10,14,12,8},{19,15,13..., dimensions={0} | all-to-all | bytes 1048576 | tf_op jit(solution)/shard_map/all_to_all | solution.py:243
  25.8 22.8 %all_to_all.41.parts_ref = f32[4,32,256]{2,1,0:T(8,128)S(1)} all-to-all(f32[4,32,256]{2,1,0:T(8,128)S(1)} %bitcast.10), channel_id=1, replica_groups={{0,20,10,30},{5,25,19,31},{4,16,14,26},{9,21,15,3},{2,22,12,24},{7,27,1..., dimensions={0} | all-to-all | bytes 262144 | tf_op jit(solution)/shard_map/all_to_all | solution.py:243
  48.6 0.0 copy-done.1
  48.6 0.2 start_kernel.1
  48.8 11.3 %all_to_all.42.parts_ref = f32[16,8,128]{2,1,0:T(8,128)S(1)} all-to-all(f32[16,8,128]{2,1,0:T(8,128)S(1)} %get-tuple-element.12), channel_id=1, replica_groups={{320,160,0,480,192,288,384,96,64,416,256,224,448,32,128,352},{321,161,1..., dimensions={0} | all-to-all | bytes 131072 | tf_op jit(solution)/shard_map/all_to_all | solution.py:243
  60.1 0.0 copy-done
  60.1 0.4 weigh_kernel.1
  60.5 15.9 %all_to_all.43 = f32[4,72,128]{2,1,0:T(8,128)S(1)} all-to-all(f32[4,72,128]{2,1,0:T(8,128)S(1)} %weigh_kernel.1), channel_id=1, replica_groups={{0,20,10,30},{27,15,21,1},{4,16,14,26},{31,11,17,5},{2,22,12,24},{29,9,..., dimensions={0} | all-to-all | bytes 294912 | tf_op jit(solution)/shard_map/all_to_all | solution.py:243
  76.5 2.0 %all-gather = f32[8,72,128]{2,1,0:T(8,128)S(1)} all-gather(f32[4,72,128]{2,1,0:T(8,128)S(1)} %all_to_all.43), channel_id=2, replica_groups={{0,1},{2,3},{4,5},{6,7},{8,9},{10,11},{12,13},{14,15},{16,17},{18,19},{..., dimensions={0}, use_global_device_ids=true | all-gather | bytes 442368 | tf_op jit(solution)/shard_map/all_gather | solution.py:257
  78.5 0.3 image_kernel.1
  78.8 9.6 %all_to_all.44.parts_ref = f32[4,32,256]{2,1,0:T(8,128)S(1)} all-to-all(f32[4,32,256]{2,1,0:T(8,128)S(1)} %image_kernel.1), channel_id=1, replica_groups={{0,4,2,6},{7,3,5,1},{20,16,22,18},{19,23,17,21},{10,14,12,8},{13,9,11,1..., dimensions={0} | all-to-all | bytes 262144 | tf_op jit(solution)/shard_map/all_to_all | solution.py:243
  88.4 0.4 project_kernel.1
  88.9 13.4 %all_to_all.45.parts_ref = f32[16,72,128]{2,1,0:T(8,128)S(1)} all-to-all(f32[16,72,128]{2,1,0:T(8,128)S(1)} %project_kernel.1), channel_id=1, replica_groups={{320,160,0,480,192,288,384,96,64,416,256,224,448,32,128,352},{321,161,1..., dimensions={0} | all-to-all | bytes 1179648 | tf_op jit(solution)/shard_map/all_to_all | solution.py:243
  102.3 1.3 %step_kernel.1 = f32[4,32,256]{2,1,0:T(8,128)S(1)} custom-call(f32[16,72,128]{2,1,0:T(8,128)S(1)} %all_to_all.45.parts_ref, f32[32,32]{1,0:T(8,128)S(1)} %copy-done, f32[2,4,72,128]{3,2,1,0:T(8,128)S(1)} %bitcast.9), custom_call_target="tpu_custom_call" | custom-call | tf_op jit(solution)/shard_map/step_kernel/pallas_call | solution.py:138
  103.6 10.2 %all_to_all.46.parts_ref = f32[4,32,256]{2,1,0:T(8,128)S(1)} all-to-all(f32[4,32,256]{2,1,0:T(8,128)S(1)} %step_kernel.1), channel_id=1, replica_groups={{0,4,2,6},{7,3,5,1},{20,16,22,18},{19,23,17,21},{10,14,12,8},{13,9,11,1..., dimensions={0} | all-to-all | bytes 262144 | tf_op jit(solution)/shard_map/all_to_all | solution.py:243
  113.7 0.3 last_kernel.1
  114.0 10.8 %all_to_all.47.parts_ref = f32[16,16,128]{2,1,0:T(8,128)S(1)} all-to-all(f32[16,16,128]{2,1,0:T(8,128)S(1)} %get-tuple-element.14), channel_id=1, replica_groups={{320,160,0,480,192,288,384,96,64,416,256,224,448,32,128,352},{321,161,1..., dimensions={0} | all-to-all | bytes 262144 | tf_op jit(solution)/shard_map/all_to_all | solution.py:243
  124.9 1.4 %finish_kernel.1 = (f32[32,256]{1,0:T(8,128)}, f32[32,32]{1,0:T(8,128)}) custom-call(f32[16,16,128]{2,1,0:T(8,128)S(1)} %all_to_all.47.parts_ref, f32[32,256]{1,0:T(8,128)S(1)} %get-tuple-element.15.image_ref, f32[32,32]{1,0:T(8,128)S(1)} %copy-done), custom_call_target="tpu_custom_call" | custom-call | tf_op jit(solution)/shard_map/finish_kernel/pallas_call | solution.py:138
  (1 shorter events, 0.0 us)
Async XLA Ops:
  0.6 48.0 %copy-start.1 = (f32[256,32]{0,1:T(8,128)S(1)}, f32[256,32]{0,1:T(8,128)}, u32[]{:S(2)}) copy-start(f32[256,32]{0,1:T(8,128)} %param.5) | copy-start | bytes 98308
  0.6 59.5 %copy-start = (f32[32,32]{1,0:T(8,128)S(1)}, f32[32,32]{1,0:T(8,128)}, u32[]{:S(2)}) copy-start(f32[32,32]{1,0:T(8,128)} %three_ref.5) | copy-start | bytes 12292
  3.9 3.8 %collective-permute-start = (f32[512,256]{1,0:T(8,128)S(1)}, f32[512,256]{1,0:T(8,128)S(1)}, u32[]{:S(2)}, u32[]{:S(2)}) collective-permute-start(f32[512,256]{1,0:T(8,128)S(1)} %get-tuple-element.11), channel_id=1, source_target_pairs={{0,1},{1,0},{2,3},{3,2},{4,5},{5,4},{6,7},{7,6},{8,9},{9,8},{10,11... | collective-permute-start | bytes 1572872 | tf_op jit(solution)/shard_map/ppermute | solution.py:249
